TPU v7x, 32 devices: a whole 2x2x4 slice. The times are simulated.
32 devices in a mesh: row: 2 (over x), col: 16 (over z, y, core).
Axes of the slice: x: 2, y: 2, z: 4, core: 2. Of those that a mesh axis runs over, the one named last changes fastest.
Arguments:
- left_features: bfloat16 [8, 1024, 320], P('row', 'col'), may hold values from -6 to 6
- right_features: bfloat16 [8, 1024, 320], P('row', 'col'), may hold values from -6 to 6
- conv_weight: bfloat16 [3, 3, 3, 40, 32], replicated, may hold values from -0.1875 to 0.1875
- cotangent: bfloat16 [24, 8, 1024, 32], P(None, 'row', 'col'), may hold values from -6 to 6
Outputs:
- cost_output: bfloat16 [24, 8, 1024, 32], P(None, 'row', 'col')
- weight_grad: float32 [3, 3, 3, 40, 32], replicated
- left_grad: bfloat16 [8, 1024, 320], P('row', 'col')
- right_grad: bfloat16 [8, 1024, 320], P('row', 'col')
All inputs are finite; a program needn't handle non-finite values.
Results may differ from a plain program's by a relative error of at most 0.0049.
Values may be sent and summed in bfloat16 or wider, within the bound.
No kernel may reach another device: no remote copies, remote signals or barrier semaphores. Data moves between devices by JAX's collectives and lax.ppermute only.
A program may use at most 128 MiB of HBM per device.

v0:
```python
import functools
import math

import jax
import jax.numpy as jnp
from jax import lax
from jax.experimental import pallas as pl
from jax.experimental.pallas import tpu as pltpu
from jax.sharding import PartitionSpec as P

DISP = 24
STEP = 4
SLOT = 64
PAD = 8
F32 = jnp.float32
BF16 = jnp.bfloat16
VMEM = pl.BlockSpec(memory_space=pltpu.VMEM)
LIMIT = 16 * 1024 * 1024


def lanes(shape):
    return lax.broadcasted_iota(jnp.int32, shape, len(shape) - 1)


def channel_table(channels, group_size, flip, value=1.0):
    shape = (group_size * SLOT, channels) if flip else (channels, group_size * SLOT)
    c = lax.broadcasted_iota(jnp.int32, shape, 1 if flip else 0)
    j = lax.broadcasted_iota(jnp.int32, shape, 0 if flip else 1)
    hit = c == (j & (SLOT - 1)) * group_size + (j >> (SLOT.bit_length() - 1))
    return jnp.where(hit, value, 0.0).astype(BF16)


def parity():
    return lax.rem(lax.axis_index("col"), 2)


def dot(a, b):
    return jnp.dot(a, b, preferred_element_type=F32)


def dot_nt(a, b):
    return lax.dot_general(a, b, (((1,), (1,)), ((), ())), preferred_element_type=F32)


def pack_kernel(ends, left, right, ct, even, odd, ctl, *rest):
    rims, ctf = rest[:-1], rest[-1]
    disp, rows, feat, cols = ct.shape
    per = 128 // feat
    for d in range(disp):
        block = ct[d].reshape(rows * feat, cols).astype(F32).T
        ctf[d * cols : (d + 1) * cols] = block
        ctl[d] = block.astype(BF16)
    columns = []
    for col in (cols - 1, 0):
        block = ctf[pl.ds(col, disp, stride=cols), :]
        block = jnp.concatenate([block, jnp.zeros((disp, left.shape[2] - rows * feat), F32)], axis=1)
        edge = [left[h, col : col + 1].astype(F32) for h in range(rows)]
        edge += [right[h, col : col + 1].astype(F32) for h in range(rows)]
        columns.append(jnp.concatenate([block, *edge], axis=0))
    is_even = parity() == 0
    even[...] = jnp.where(is_even, columns[0], columns[1]).astype(BF16)
    odd[...] = jnp.where(is_even, columns[1], columns[0]).astype(BF16)
    for end, rim in zip(ends, rims):
        h = end()
        for q in range(disp // per):
            rim[q, PAD : PAD + cols] = jnp.concatenate(
                [ct[q * per + i, h].astype(F32) for i in range(per)], axis=0
            ).T


def pass_kernel(own, got, end, out, end_out):
    end_out[...] = end[...]
    out[...] = jnp.where(parity() == 0, own[...].astype(F32), got[...].astype(F32)).astype(BF16)


def end_columns(by_even, by_odd):
    x, y = by_even[...].astype(F32), by_odd[...].astype(F32)
    is_even = parity() == 0
    return jnp.where(is_even, y, x), jnp.where(is_even, x, y)


def row_kernel(ends, rows, by_even, by_odd, *rest):
    n = len(ends)
    rims, pays, (edges, buf) = rest[:n], rest[n : 2 * n], rest[2 * n :]
    count, total, _ = buf.shape
    disp = edges.shape[1]
    per, cols = disp // count, total - 2 * PAD
    feat = 128 // per
    lane = lanes((count, 128))
    for side, x in enumerate(end_columns(by_even, by_odd)):
        edges[side] = x[0:disp, 0:128]
    for end, rim, pay in zip(ends, rims, pays):
        h = end()
        buf[...] = rim[...]
        for side, at in ((0, PAD - 1), (1, PAD + cols)):
            out = jnp.zeros((count, 128), F32)
            for i in range(per):
                x = edges[side, pl.ds(i, count, stride=per)]
                first = pltpu.roll(x, feat * i, 1) if i else x
                last = pltpu.roll(x, (feat * (i - rows + 1)) % 128, 1) if i != rows - 1 else x
                x = jnp.where(h == 0, first, last)
                out = jnp.where((lane >= feat * i) & (lane < feat * (i + 1)), x, out)
            for q in range(count):
                buf[q, at : at + 1] = out[q : q + 1]
        pay[...] = buf[...].astype(BF16)


def volume_kernel(ends, group_size, left, right, near, far, by_even, by_odd, vbuf, fl, fr, fr4, *rest):
    pays, (mixed, wide_buf) = rest[: len(ends)], rest[len(ends) :]
    rows, cols, channels = left.shape
    disp = vbuf.shape[1]
    reach = fr.shape[1] - cols - PAD
    wide = group_size * SLOT
    base, half = rows * cols, cols // 2
    mixed[0:base] = near[...].reshape(base, channels)
    mixed[base : 2 * base] = right[...].reshape(base, channels)
    mixed[2 * base : 3 * base] = left[...].reshape(base, channels)
    at_far, at_ends = 3 * base, 3 * base + base // 2
    mixed[at_far:at_ends] = far[:, half:].reshape(base // 2, channels)
    count = disp + 2 * rows
    for i, x in enumerate(end_columns(by_even, by_odd)):
        mixed[at_ends + i * count : at_ends + (i + 1) * count] = x.astype(BF16)
    wide_buf[...] = dot(mixed[...], channel_table(channels, group_size, False))
    scale = 1.0 / group_size
    for h in range(rows):
        fl[h, 0:PAD] = jnp.zeros((PAD, wide), F32)
        fl[h, PAD + cols :] = jnp.zeros((PAD, wide), F32)
        at = at_ends + disp + h
        fl[h, PAD - 1 : PAD] = wide_buf[at : at + 1] * scale
        fl[h, PAD : PAD + cols] = wide_buf[2 * base + h * cols : 2 * base + (h + 1) * cols] * scale
        at += count
        fl[h, PAD + cols : PAD + cols + 1] = wide_buf[at : at + 1] * scale
        for ref, off in ((fr, 0), (fr4, STEP)):
            start = reach - cols - half + off
            ref[h, 0:start] = jnp.zeros((start, wide), F32)
            ref[h, start : start + half] = wide_buf[at_far + h * half : at_far + (h + 1) * half]
            for part in range(2):
                at = part * base + h * cols
                to = start + half + part * cols
                ref[h, to : to + cols] = wide_buf[at : at + cols]
            to = start + half + 2 * cols
            ref[h, to:] = jnp.zeros((ref.shape[1] - to, wide), F32)
            at = at_ends + count + disp + rows + h
            ref[h, to : to + 1] = wide_buf[at : at + 1]
    total = cols + 2 * PAD
    low = lanes((8, 128)) < SLOT
    pairs, times, lots = rows // 2, disp // 2, wide // 128
    count = total // 16

    def products(i, _):
        p, at = lax.rem(i, pairs), pl.multiple_of(lax.div(i, pairs) * (8 * count), 8)
        lefts = [
            [
                [fl[2 * p + o, pl.ds(at + 8 * b, 8), 128 * j : 128 * (j + 1)] for j in range(lots)]
                for b in range(count)
            ]
            for o in range(2)
        ]
        for odd, band in enumerate((fr, fr4)):
            for r in range(1 - times, count):
                start = pl.multiple_of(at + reach - PAD + 8 * r, 8)
                here = [
                    [band[2 * p + o, pl.ds(start, 8), 128 * j : 128 * (j + 1)] for j in range(lots)]
                    for o in range(2)
                ]
                for t in range(max(0, -r), min(times, count - r)):
                    sums = []
                    for o in range(2):
                        acc = lefts[o][r + t][0] * here[o][0]
                        for j in range(1, lots):
                            acc = acc + lefts[o][r + t][j] * here[o][j]
                        sums.append(acc + pltpu.roll(acc, SLOT, 1))
                    vbuf[p, 2 * t + odd, pl.ds(at + 8 * (r + t), 8)] = jnp.where(low, *sums)
        return 0

    lax.fori_loop(0, 2 * pairs, products, 0)
    big = lanes((total, 128)) < SLOT

    for dd in range(disp // 2):
        for end, pay in zip(ends, pays):
            h = end()
            if isinstance(h, int):
                halves = [vbuf[h // 2, 2 * dd + o] for o in range(2)]
                if h % 2 == 0:
                    halves[1] = pltpu.roll(halves[1], SLOT, 1)
                else:
                    halves[0] = pltpu.roll(halves[0], SLOT, 1)
                out = jnp.where(big, halves[0], halves[1])
            else:
                last = pairs - 1
                first = jnp.where(big, vbuf[0, 2 * dd], pltpu.roll(vbuf[0, 2 * dd + 1], SLOT, 1))
                final = jnp.where(
                    big, pltpu.roll(vbuf[last, 2 * dd], SLOT, 1), vbuf[last, 2 * dd + 1]
                )
                out = jnp.where(h == 0, first, final)
            pay[dd * total : (dd + 1) * total] = out.astype(BF16)


def weight_kernel(masks, groups, vbuf, ctl, by_even, by_odd, top, bot, keep_out, give_out, ctsh, vt, buf, sums):
    disp, cols, width = ctl.shape
    rows, feat = 2 * vbuf.shape[0], 32
    per = 128 // feat
    mtop, mbot = masks()
    ctsh[0] = jnp.zeros(ctsh.shape[1:], BF16)
    ctsh[disp + 1] = jnp.zeros(ctsh.shape[1:], BF16)
    lane = lanes(top.shape[1:])
    edges = [x[0:disp, 0:128] for x in end_columns(by_even, by_odd)]
    for d in range(disp):
        buf[d, PAD - 1 : PAD, 0:128] = edges[0][d : d + 1]
        buf[d, PAD + cols : PAD + cols + 1, 0:128] = edges[1][d : d + 1]

    def fill(q, _):
        t = top[q].astype(F32) * mtop
        z = bot[q].astype(F32) * mbot
        for i in range(per):
            d = q * per + i
            a = t if i == 0 else pltpu.roll(t, 128 - feat * i, 1)
            y = z if i == 1 else pltpu.roll(z, (128 + feat - feat * i) % 128, 1)
            buf[d, PAD : PAD + cols, 0:128] = ctl[d].astype(F32)
            buf[d, :, 128:256] = jnp.where(lane < feat, a, jnp.where(lane < 2 * feat, y, 0.0))
            for e in range(3):
                ctsh[d + 1, :, 256 * e : 256 * (e + 1)] = buf[
                    d, PAD - 1 + e : PAD - 1 + e + cols
                ].astype(BF16)
        return 0

    lax.fori_loop(0, disp // per, fill, 0, unroll=True)
    step = 256 // cols
    for q in range(disp // step):
        for p in range(rows // 2):
            v = vbuf[p, q * step : (q + 1) * step, PAD : PAD + cols].reshape(256, 128).astype(BF16)
            vt[128 * p : 128 * (p + 1), 256 * q : 256 * (q + 1)] = v.T
    keep = lanes((groups, 128))
    sums[...] = jnp.zeros(sums.shape, F32)

    def taps(a, _):
        for e in range(3):
            ct_block = ctsh[pl.ds(a, disp), :, 256 * e : 256 * (e + 1)].reshape(disp * cols, 256)
            full = dot(vt[...], ct_block)
            out = None
            for h in range(rows):
                x = full[SLOT * h : SLOT * h + groups, 0:128]
                y = full[SLOT * h : SLOT * h + groups, 128:256]
                if h == 0:
                    term = jnp.where(keep < feat, y, pltpu.roll(x, feat, 1))
                else:
                    term = x if h == 1 else pltpu.roll(x, 128 - feat * (h - 1), 1)
                    if h == rows - 1:
                        term = jnp.where(keep < 2 * feat, term, pltpu.roll(y, feat, 1))
                out = term if out is None else out + term
            at = pl.multiple_of(a * 128 + groups * e, 8)
            sums[pl.ds(at, groups)] = jnp.where(keep < 3 * feat, out, 0.0)
        return 0

    lax.fori_loop(0, 3, taps, 0)
    half = sums.shape[0] // 2
    is_even = parity() == 0
    low, high = sums[0:half], sums[half:]
    keep_out[...] = jnp.where(is_even, low, high)
    give_out[...] = jnp.where(is_even, high, low)


def right_kernel(ctsh, w2, fl, gv, rg0, rg1, rg2, acce, acco, both):
    disp = ctsh.shape[0] - 2
    rows, cols, channels = rg0.shape
    wide = fl.shape[2]
    group_size = wide // SLOT
    step = 512 // cols
    low = lanes((512, 128)) < SLOT

    def conv(q, _):
        slabs = [ctsh[pl.ds(q * step + a, step)].reshape(512, ctsh.shape[2]) for a in range(3)]
        acc = dot(jnp.concatenate(slabs, axis=1), w2[...])
        g = acc.astype(BF16).astype(F32)
        for p in range(rows // 2):
            x = g[:, 128 * p : 128 * (p + 1)]
            r = pltpu.roll(x, SLOT, 1)
            for o in range(2):
                y = jnp.where(low, r, x) if o else jnp.where(low, x, r)
                gv[2 * p + o, pl.ds(q * step, step)] = y.reshape(step, cols, 128)
        return 0

    lax.fori_loop(0, disp // step, conv, 0)
    count = cols // 8
    back = acce.shape[1] - cols
    lead = back // 8

    lots = wide // 128

    def right_row(h, _):
        here = [
            [fl[h, PAD + 8 * b : PAD + 8 * b + 8, 128 * j : 128 * (j + 1)] for j in range(lots)]
            for b in range(count)
        ]
        for odd, buf in enumerate((acce, acco)):
            for k in range(lead + count):
                accs = [None] * lots
                for t in range(disp // 2):
                    b = k + t - lead
                    if b < 0 or b >= count:
                        continue
                    g = gv[h, 2 * t + odd, 8 * b : 8 * b + 8]
                    for j in range(lots):
                        term = g * here[b][j]
                        accs[j] = term if accs[j] is None else accs[j] + term
                for j in range(lots):
                    x = jnp.zeros((8, 128), F32) if accs[j] is None else accs[j]
                    buf[h, 8 * k : 8 * k + 8, 128 * j : 128 * (j + 1)] = x
        acco[h, 8 * (lead + count) :] = jnp.zeros((8, wide), F32)
        return 0

    lax.fori_loop(0, rows, right_row, 0)
    size = back + cols
    for h in range(rows):
        both[h * size : (h + 1) * size] = (acce[h] + acco[h, STEP : STEP + size]).astype(BF16)
    whole = dot(both[...], channel_table(channels, group_size, True)).astype(BF16)
    half = cols // 2
    for h in range(rows):
        at = h * size + back
        rg2[h] = whole[at - cols - half : at - cols]
        rg1[h] = whole[at - cols : at]
        rg0[h] = whole[at : at + cols]


def left_kernel(gv, fr, fr4, lg, accl):
    rows, cols, channels = lg.shape
    disp, wide = gv.shape[1], fr.shape[2]
    group_size = wide // SLOT
    reach = fr.shape[1] - cols - PAD
    count, times, lots = cols // 8, disp // 2, wide // 128

    def left_row(h, _):
        accs = [[None] * lots for _ in range(count)]
        for odd, band in enumerate((fr, fr4)):
            for r in range(1 - times, count):
                at = reach + 8 * r
                here = [band[h, at : at + 8, 128 * j : 128 * (j + 1)] for j in range(lots)]
                for t in range(max(0, -r), min(times, count - r)):
                    g = gv[h, 2 * t + odd, 8 * (r + t) : 8 * (r + t) + 8]
                    for j in range(lots):
                        term, acc = g * here[j], accs[r + t][j]
                        accs[r + t][j] = term if acc is None else acc + term
        for b in range(count):
            for j in range(lots):
                accl[h, 8 * b : 8 * b + 8, 128 * j : 128 * (j + 1)] = accs[b][j] * (1.0 / group_size)
        return 0

    lax.fori_loop(0, rows, left_row, 0)
    whole = accl[...].reshape(rows * cols, wide).astype(BF16)
    out = dot(whole, channel_table(channels, group_size, True)).astype(BF16)
    lg[...] = out.reshape(rows, cols, channels)


def combine_kernel(got, rg2, out):
    cols = out.shape[1]
    half = cols // 2
    part = jnp.where(parity() == 0, 0.0, got[...].astype(F32))
    out[:, 0:half] = part[:, 0:half].astype(BF16)
    out[:, half:] = (part[:, half:] + rg2[...].astype(F32)).astype(BF16)


def halo_lanes(groups):
    first = SLOT - groups
    assert groups - first <= first
    return (groups, SLOT, groups), (SLOT + groups, SLOT + 2 * groups - first, SLOT + groups - first)


def place_halo(base, row, groups, offset, lane):
    for start, end, shift in halo_lanes(groups):
        moved = pltpu.roll(row, (shift - offset) % 128, 1)
        base = jnp.where((lane >= start) & (lane < end), moved, base)
    return base


def conv_kernel(masks, groups, vbuf, top, bot, wc, out, taps, buf):
    disp, rows, feat, cols = out.shape
    total = buf.shape[2]
    lane = lanes((total, 128))
    zeros = jnp.zeros((cols, taps.shape[3]), BF16)
    taps[0, 0] = zeros
    taps[disp // 2, 1] = zeros
    halos_of = [(ref, mask) for ref, mask in zip((top, bot), masks())]
    for dd in range(disp // 2):
        for p, (ref, mask) in enumerate(halos_of):
            row = ref[dd * total : (dd + 1) * total].astype(F32) * mask
            for o in range(2):
                d = 2 * dd + o
                buf[p, d] = place_halo(vbuf[p, d], row, groups, SLOT * o, lane)
                for e in range(3):
                    at = 256 * e + 128 * p
                    taps[(d + 1) // 2, (d + 1) % 2, :, at : at + 128] = buf[
                        p, d, PAD - 1 + e : PAD - 1 + e + cols
                    ].astype(BF16)
    step = 6

    def conv(q, _):
        slabs = [
            taps[pl.ds(q * step + s // 2, step), s % 2].reshape(step * cols, taps.shape[3])
            for s in range(4)
        ]
        acc = dot(jnp.concatenate(slabs, axis=1), wc[...])
        for j in range(step):
            both = acc[j * cols : (j + 1) * cols].T.astype(BF16)
            for o in range(2):
                block = both[rows * feat * o : rows * feat * (o + 1)]
                out[2 * (q * step + j) + o] = block.reshape(rows, feat, cols)
        return 0

    lax.fori_loop(0, disp // 2 // step, conv, 0)


def finish_kernel(scale, mine, other, own, near, far, weight, right):
    _, _, _, feat, groups = weight.shape
    is_even = parity() == 0
    x, y = mine[...] * scale, other[...] * scale
    total = jnp.concatenate([jnp.where(is_even, x, y), jnp.where(is_even, y, x)], axis=0)
    for a in range(3):
        for e in range(3):
            at = 128 * a + groups * e
            block = total[at : at + groups].T
            for b in range(3):
                weight[2 - a, 2 - b, 2 - e] = block[feat * b : feat * (b + 1)]
    beside = jnp.where(is_even, near[...].astype(F32), 0.0)
    right[...] = (own[...].astype(F32) + beside + far[...].astype(F32)).astype(BF16)


def sum_kernel(*refs):
    *parts, out = refs
    out[...] = tree([ref[...].astype(F32) for ref in parts]).astype(out.dtype)


def tree(terms):
    while len(terms) > 1:
        terms = [terms[i] + terms[i + 1] for i in range(0, len(terms), 2)]
    return terms[0]


def taps_kernel(taps, w2, wc, turned):
    _, _, _, feat, groups = taps.shape
    rows = wc.shape[1] // 2 // feat
    lane_of = lanes((feat, 2 * SLOT))
    low = lanes((feat, 2 * SLOT)) < SLOT
    zero = jnp.zeros((feat, 2 * SLOT), F32)

    def wide(a, b, e):
        if not 0 <= b <= 2:
            return None
        return jnp.concatenate([taps[a, b, e].astype(F32), zero[:, groups:]], axis=1)

    def beside(x, y):
        if x is None and y is None:
            return zero
        x = zero if x is None else x
        y = zero if y is None else pltpu.roll(y, SLOT, 1)
        return jnp.where(low, x, y)

    def build(a, _):
        def at_row(h):
            return pl.multiple_of((a * rows + h) * feat, feat)

        def at_tap(row):
            return pl.multiple_of(a * 3 * 256 + row, feat)

        for e in range(3):
            for h in range(rows):
                for p in range(rows // 2):
                    lane = SLOT * (rows * e + 2 * p)
                    block = beside(wide(a, 2 * p - h + 1, e), wide(a, 2 * p + 1 - h + 1, e))
                    if h == 0 and p == 0:
                        block = place_halo(block, wide(a, 0, e), groups, 0, lane_of)
                    if h == rows - 1 and p == rows // 2 - 1:
                        block = place_halo(block, wide(a, 2, e), groups, 0, lane_of)
                    turned[pl.ds(at_row(h), feat), lane : lane + 2 * SLOT] = block
            for slot, six in enumerate((*range(1, rows + 1), 0, rows + 1)):
                at = 256 * e + feat * slot
                for p in range(rows // 2):
                    back = [2 - (six - 2 * p - o) for o in range(2)]
                    w2[pl.ds(at_tap(at), feat), 2 * SLOT * p : 2 * SLOT * (p + 1)] = beside(
                        wide(2 - a, back[0], 2 - e), wide(2 - a, back[1], 2 - e)
                    ).astype(BF16)
            at = 256 * e + feat * (rows + 2)
            size = 256 - feat * (rows + 2)
            w2[pl.ds(at_tap(at), size)] = jnp.zeros((size, rows * SLOT), BF16)
        return 0

    lax.fori_loop(0, 3, build, 0)
    depth, size = turned.shape[1], rows * feat
    for a in range(3):
        for i in range(depth // 128):
            x = turned[size * a : size * (a + 1), 128 * i : 128 * (i + 1)].T.astype(BF16)
            for o in range(2):
                at = depth * (a + o) + 128 * i
                wc[at : at + 128, size * o : size * (o + 1)] = x
    for o in range(2):
        at = depth * 3 * (1 - o)
        wc[at : at + depth, size * o : size * (o + 1)] = jnp.zeros((depth, size), BF16)


TOKEN = ((8, 128), F32)


def with_token(kernel, inputs, outputs):
    def run(*refs):
        kernel(*refs[: inputs + outputs], *refs[inputs + outputs + 1 :])
        refs[inputs + outputs][...] = jnp.zeros(TOKEN[0], F32)

    return run


def call(kernel, outs, scratch, *args, after=(), token=False, us=0.0):
    skip = len(after)
    if token:
        kernel = with_token(kernel, len(args), len(outs))
        outs = [*outs, TOKEN]
    return pl.pallas_call(
        lambda *refs: kernel(*refs[skip:]),
        out_shape=[jax.ShapeDtypeStruct(s, t) for s, t in outs],
        in_specs=[pl.BlockSpec(memory_space=pl.ANY)] * skip + [VMEM] * len(args),
        out_specs=[VMEM] * len(outs),
        scratch_shapes=scratch,
        compiler_params=pltpu.CompilerParams(vmem_limit_bytes=LIMIT),
        cost_estimate=pl.CostEstimate(
            flops=int(us * 1.15e9), bytes_accessed=int(us * 3.7e6), transcendentals=0
        ),
    )(*after, *args)


def col_shift(block, distance):
    n = lax.axis_size("col")
    route = [(i - distance, i) for i in range(n) if 0 <= i - distance < n]
    return lax.ppermute(block, "col", route)


def row_shift(block, distance):
    n = lax.axis_size("row")
    route = [(i - distance, i) for i in range(n) if 0 <= i - distance < n]
    return lax.ppermute(block, "row", route)


def halos(pays):
    if lax.axis_size("row") == 2:
        got = lax.ppermute(pays[0], "row", [(0, 1), (1, 0)])
        return got, got
    return row_shift(pays[0], 1), row_shift(pays[1], -1)


def stages(n_row, n_col):
    col_bits = [1 << i for i in range(1, n_col.bit_length() - 1)]
    row_bits = [n_col << i for i in range(n_row.bit_length() - 1)]
    assert n_col == 2 << len(col_bits) and n_row == 1 << len(row_bits)
    bits = col_bits[:1] + row_bits + col_bits[1:]
    out = []
    for i in range(0, len(bits), 2):
        pair = bits[i : i + 2]
        out.append(pair + [sum(pair)] if len(pair) == 2 else pair)
    return out


def on_device(left_features, right_features, conv_weight, cotangent):
    rows, cols, channels = left_features.shape
    disp, feat = cotangent.shape[0], cotangent.shape[3]
    groups = conv_weight.shape[3]
    group_size = channels // groups
    wide = group_size * SLOT
    n_row, n_col = lax.axis_size("row"), lax.axis_size("col")
    per = 128 // feat

    if n_row == 2:
        ends = [lambda: (rows - 1) * (1 - lax.axis_index("row"))]
    else:
        ends = [lambda: rows - 1, lambda: 0]
    n = len(ends)

    def masks():
        at = lax.axis_index("row")
        return (
            jnp.where(at > 0, 1.0, 0.0).astype(F32),
            jnp.where(at < n_row - 1, 1.0, 0.0).astype(F32),
        )

    total = cols + 2 * PAD
    count = disp + 2 * rows
    ct = cotangent.transpose(0, 1, 3, 2)

    def swap(block, mask):
        route = [(i, i ^ mask) for i in range(n_row * n_col)]
        return lax.ppermute(block, ("row", "col"), route)

    far = col_shift(right_features, 2)
    by_even, by_odd, ctl, *rims = call(
        functools.partial(pack_kernel, ends),
        [
            ((count, channels), BF16),
            ((count, channels), BF16),
            ((disp, cols, rows * feat), BF16),
        ]
        + [((disp // per, total, 128), F32)] * n,
        [pltpu.VMEM((disp * cols, rows * feat), F32)],
        left_features,
        right_features,
        ct,
        us=0.4,
    )
    by_even = swap(by_even, 1)
    near, by_odd = call(
        pass_kernel,
        [((rows, cols, channels), BF16), ((count, channels), BF16)],
        [],
        right_features,
        far,
        by_odd,
    )
    near = swap(near, 1)
    inner = range(1, n_col - 1, 2)
    by_odd = lax.ppermute(by_odd, "col", [(i, i + 1) for i in inner] + [(i + 1, i) for i in inner])
    row_pays = call(
        functools.partial(row_kernel, ends, rows),
        [((disp // per, total, 128), BF16)] * n,
        [pltpu.VMEM((2, disp, 128), F32), pltpu.VMEM((disp // per, total, 128), F32)],
        by_even,
        by_odd,
        *rims,
    )
    top, bot = halos(row_pays)

    band = 104 + cols + PAD
    spread_rows = 3 * rows * cols + rows * cols // 2 + 2 * count
    vbuf, fl, fr, fr4, *volume_rows = call(
        functools.partial(volume_kernel, ends, group_size),
        [
            ((rows // 2, disp, total, 2 * SLOT), F32),
            ((rows, total, wide), F32),
            ((rows, band, wide), F32),
            ((rows, band, wide), F32),
        ]
        + [((disp // 2 * total, 128), BF16)] * n,
        [
            pltpu.VMEM((spread_rows, channels), BF16),
            pltpu.VMEM((spread_rows, wide), F32),
        ],
        left_features,
        right_features,
        near,
        far,
        by_even,
        by_odd,
        after=row_pays,
        us=2.3,
    )
    vtop, vbot = halos(volume_rows)

    keep, give, ctsh = call(
        functools.partial(weight_kernel, masks, groups),
        [((3 * 64, 128), F32), ((3 * 64, 128), F32), ((disp + 2, cols, 3 * 256), BF16)],
        [
            pltpu.VMEM((rows * SLOT, disp * cols), BF16),
            pltpu.VMEM((disp, total, 256), F32),
            pltpu.VMEM((3 * 128, 128), F32),
        ],
        vbuf, ctl, by_even, by_odd, top, bot,
        us=3.4,
    )
    got = swap(give, 1)
    w2, wc = call(
        taps_kernel,
        [((9 * 256, rows * SLOT), BF16), ((4 * 3 * rows * SLOT, 2 * rows * feat), BF16)],
        [pltpu.VMEM((3 * rows * feat, 3 * rows * SLOT), F32)],
        conv_weight.transpose(0, 1, 2, 4, 3),
        after=[keep],
        us=0.8,
    )
    (part,) = call(sum_kernel, [(keep.shape, BF16)], [], keep, got, after=[w2])
    gv, rg0, rg1, rg2 = call(
        right_kernel,
        [
            ((rows, disp, cols, 128), F32),
            ((rows, cols, channels), BF16),
            ((rows, cols, channels), BF16),
            ((rows, cols // 2, channels), BF16),
        ],
        [
            pltpu.VMEM((rows, cols + cols + cols // 2, wide), F32),
            pltpu.VMEM((rows, cols + cols + cols // 2 + 8, wide), F32),
            pltpu.VMEM((rows * (cols + cols + cols // 2), wide), BF16),
        ],
        ctsh, w2, fl,
        after=[part],
        us=3.8,
    )
    rg1 = swap(rg1, 1)
    *middle, final = stages(n_row, n_col)
    order = [rg0]
    for stage in middle:
        parts = [part] + [swap(part, m) for m in stage]
        (part,) = call(sum_kernel, [(part.shape, BF16)], [], *parts, after=order)
        order = []
    parts = [part] + [swap(part, m) for m in final]
    (rg2,) = call(
        combine_kernel, [((rows, cols, channels), BF16)], [], rg1, rg2, after=[part]
    )
    output, conv_done = call(
        functools.partial(conv_kernel, masks, groups),
        [((disp, rows, feat, cols), BF16)],
        [
            pltpu.VMEM((disp // 2 + 1, 2, cols, 3 * rows * SLOT), BF16),
            pltpu.VMEM((rows // 2, disp, total, 128), F32),
        ],
        vbuf, vtop, vbot, wc,
        after=[part, rg2],
        token=True,
        us=3.8,
    )
    (part,) = call(sum_kernel, [(part.shape, F32)], [], *parts, after=[conv_done])
    lg, left_done = call(
        left_kernel,
        [((rows, cols, channels), BF16)],
        [pltpu.VMEM((rows, cols, wide), F32)],
        gv, fr, fr4,
        after=[part],
        token=True,
        us=1.9,
    )
    rg2 = col_shift(rg2, -2)
    cells = disp * rows * n_row * cols * n_col
    weight_grad, right_grad = call(
        functools.partial(finish_kernel, 1.0 / math.sqrt(cells)),
        [((3, 3, 3, feat, groups), F32), ((rows, cols, channels), BF16)],
        [],
        part, swap(part, 1), rg0, rg1, rg2,
        after=[left_done],
        us=1.0,
    )
    return (
        output.transpose(0, 1, 3, 2),
        weight_grad.transpose(0, 1, 2, 4, 3),
        lg,
        right_grad,
    )


def solution(mesh):
    in_specs = (P("row", "col", None), P("row", "col", None), P(), P(None, "row", "col", None))
    out_specs = (P(None, "row", "col", None), P(), P("row", "col", None), P("row", "col", None))
    return jax.shard_map(
        on_device, mesh=mesh, in_specs=in_specs, out_specs=out_specs, check_vma=False
    )
```

profile of v0, /device:TPU:0, one launch (start us, length us, event | category | flops | bytes accessed | tf_op | source)
XLA Modules:
  0.0 53.4 jit_solution(2267399846416190618)
XLA Ops:
  0.6 4.9 %collective-permute-start.1 = (bf16[4,64,320]{2,1,0:T(8,128)(2,1)}, bf16[4,64,320]{2,1,0:T(8,128)(2,1)S(1)}, u32[]{:S(2)}, u32[]{:S(2)}) collective-permute-start(bf16[4,64,320]{2,1,0:T(8,128)(2,1)} %refs_2_.1), channel_id=1, source_target_pairs={{0,2},{1,3},{2,4},{3,5},{4,6},{5,7},{6,8},{7,9},{8,10},{9,11},{10,... | collective-permute-start | bytes 491528 | tf_op jit(solution)/shard_map/ppermute | solution.py:531
  5.5 0.0 copy-start
  5.5 0.9 %copy-done = bf16[4,64,320]{2,1,0:T(8,128)(2,1)S(1)} copy-done((bf16[4,64,320]{2,1,0:T(8,128)(2,1)S(1)}, bf16[4,64,320]{2,1,0:T(8,128)(2,1)}, u32[]{:S(2)}) %copy-start) | copy-done | bytes 163864
  6.5 0.0 copy-start.2
  6.5 1.1 %copy-done.2 = bf16[24,4,64,32]{2,3,1,0:T(8,128)(2,1)S(1)} copy-done((bf16[24,4,64,32]{2,3,1,0:T(8,128)(2,1)S(1)}, bf16[24,4,64,32]{2,3,1,0:T(8,128)(2,1)}, u32[]{:S(2)}) %copy-start.2) | copy-done | bytes 393240
  7.6 0.0 copy-start.4
  7.6 0.9 %copy-done.4 = bf16[4,64,320]{2,1,0:T(8,128)(2,1)S(1)} copy-done((bf16[4,64,320]{2,1,0:T(8,128)(2,1)S(1)}, bf16[4,64,320]{2,1,0:T(8,128)(2,1)}, u32[]{:S(2)}) %copy-start.4) | copy-done | bytes 163864
  8.5 0.0 copy-start.1
  8.5 0.3 shard_map.75
  8.8 1.1 %collective-permute-done.1.refs_1_.refs_4_ = bf16[4,64,320]{2,1,0:T(8,128)(2,1)S(1)} collective-permute-done((bf16[4,64,320]{2,1,0:T(8,128)(2,1)}, bf16[4,64,320]{2,1,0:T(8,128)(2,1)S(1)}, u32[]{:S(2)}, u32[]{:S(2)}) %collective-permute-start.1) | collective-permute-done | bytes 163872 | tf_op jit(solution)/shard_map/ppermute | solution.py:531
  10.0 0.0 copy-done.1
  10.0 0.1 shard_map.76
  10.0 0.1 collective-permute-start.3
  10.1 0.5 collective-permute-start
  10.6 0.7 %collective-permute-start.2 = (bf16[32,320]{1,0:T(8,128)(2,1)S(1)}, bf16[32,320]{1,0:T(8,128)(2,1)S(1)}, u32[]{:S(2)}, u32[]{:S(2)}) collective-permute-start(bf16[32,320]{1,0:T(8,128)(2,1)S(1)} %get-tuple-element.32), channel_id=1, source_target_pairs={{1,2},{3,4},{5,6},{7,8},{9,10},{11,12},{13,14},{2,1},{4,3},{6,5},{... | collective-permute-start | bytes 61448 | tf_op jit(solution)/shard_map/ppermute | solution.py:615
  11.3 0.3 collective-permute-done.refs_0_.refs_5_.refs_2_
  11.6 0.0 collective-permute-done.2.refs_1_.refs_6_.refs_3_
  11.6 0.1 shard_map.77.refs_0_
  11.7 1.6 %collective-permute-start.4 = (bf16[6,80,128]{2,1,0:T(8,128)(2,1)S(1)}, bf16[6,80,128]{2,1,0:T(8,128)(2,1)S(1)}, u32[]{:S(2)}, u32[]{:S(2)}) collective-permute-start(bf16[6,80,128]{2,1,0:T(8,128)(2,1)S(1)} %shard_map.77.refs_0_), channel_id=1, source_target_pairs={{0,16},{16,0},{1,17},{17,1},{2,18},{18,2},{3,19},{19,3},{4,20},{20... | collective-permute-start | bytes 368648 | tf_op jit(solution)/shard_map/ppermute | solution.py:542
  13.2 0.0 collective-permute-done.3.refs_3_
  13.2 2.4 %shard_map.78 = (f32[2,24,80,128]{3,2,1,0:T(8,128)S(1)}, f32[4,80,512]{2,1,0:T(8,128)S(1)}, f32[4,176,512]{2,1,0:T(8,128)S(1)}, f32[4,176,512]{2,1,0:T(8,128)S(1)}, bf16[960,128]{1,0:T(8,128)(2,1)S(1)}) custom-call(bf16[6,80,128]{2,1,0:T(8,128)(2,1)S(1)} %shard_map.77.refs_0_, bf16[4,64,320]{2,1,0:T(8,128)(2,1)S(1)} %copy-done.4, ...), custom_call_target="tpu_custom_call" | custom-call | flops 2644999936 | bytes 8510000 | tf_op jit(solution)/shard_map/pallas_call | solution.py:515
  15.6 1.0 %collective-permute-done.4.refs_4_.refs_5_ = bf16[6,80,128]{2,1,0:T(8,128)(2,1)S(1)} collective-permute-done((bf16[6,80,128]{2,1,0:T(8,128)(2,1)S(1)}, bf16[6,80,128]{2,1,0:T(8,128)(2,1)S(1)}, u32[]{:S(2)}, u32[]{:S(2)}) %collective-permute-start.4) | collective-permute-done | bytes 122912 | tf_op jit(solution)/shard_map/ppermute | solution.py:542
  16.6 0.0 copy-start.3
  16.6 3.5 %shard_map.79 = (f32[192,128]{1,0:T(8,128)S(1)}, f32[192,128]{1,0:T(8,128)S(1)}, bf16[26,64,768]{2,1,0:T(8,128)(2,1)S(1)}) custom-call(f32[2,24,80,128]{3,2,1,0:T(8,128)S(1)} %get-tuple-element.35.refs_0_.refs_2_, bf16[24,64,128]{2,1,0:T(8,128)(2,1)S(1)} %get-tuple-element.36.refs_1_, bf16[32,320]{1,0:T(8,128)(2,1)S(1)} %collective-permute-done.refs_0_.refs_5_.refs_2_, ...), custom_call_target="tpu_custom_call" | custom-call | flops 3910000128 | bytes 12580000 | tf_op jit(solution)/shard_map/pallas_call | solution.py:515
  20.1 4.1 %collective-permute-start.5 = (f32[192,128]{1,0:T(8,128)S(1)}, f32[192,128]{1,0:T(8,128)S(1)}, u32[]{:S(2)}, u32[]{:S(2)}) collective-permute-start(f32[192,128]{1,0:T(8,128)S(1)} %get-tuple-element.39), channel_id=1, source_target_pairs={{0,1},{1,0},{2,3},{3,2},{4,5},{5,4},{6,7},{7,6},{8,9},{9,8},{10,11... | collective-permute-start | bytes 294920 | tf_op jit(solution)/shard_map/ppermute | solution.py:587
  24.2 1.5 %collective-permute-start.10 = (bf16[960,128]{1,0:T(8,128)(2,1)S(1)}, bf16[960,128]{1,0:T(8,128)(2,1)S(1)}, u32[]{:S(2)}, u32[]{:S(2)}) collective-permute-start(bf16[960,128]{1,0:T(8,128)(2,1)S(1)} %get-tuple-element.45), channel_id=1, source_target_pairs={{0,16},{16,0},{1,17},{17,1},{2,18},{18,2},{3,19},{19,3},{4,20},{20... | collective-permute-start | bytes 737288 | tf_op jit(solution)/shard_map/ppermute | solution.py:542
  25.7 0.0 copy-done.3
  25.7 0.8 %shard_map.80 = (bf16[2304,256]{1,0:T(8,128)(2,1)S(1)}, bf16[3072,256]{1,0:T(8,128)(2,1)S(1)}) custom-call(f32[192,128]{1,0:T(8,128)S(1)} %get-tuple-element.37.refs_0_.refs_1_, bf16[3,3,3,32,40]{4,3,2,1,0:T(8,128)(2,1)S(1)} %bitcast.5), custom_call_target="tpu_custom_call" | custom-call | flops 920000000 | bytes 2960000 | tf_op jit(solution)/shard_map/pallas_call | solution.py:515
  26.5 0.0 collective-permute-done.5.refs_2_
  26.5 3.9 %shard_map.82 = (f32[4,24,64,128]{3,2,1,0:T(8,128)S(1)}, bf16[4,64,320]{2,1,0:T(8,128)(2,1)S(1)}, bf16[4,64,320]{2,1,0:T(8,128)(2,1)S(1)}, bf16[4,32,320]{2,1,0:T(8,128)(2,1)S(1)}) custom-call(bf16[192,128]{1,0:T(8,128)(2,1)S(1)} %shard_map.81.refs_0_.refs_1_, bf16[26,64,768]{2,1,0:T(8,128)(2,1)S(1)} %get-tuple-element.40.refs_1_, ...), custom_call_target="tpu_custom_call" | custom-call | flops 4369999872 | bytes 14060000 | tf_op jit(solution)/shard_map/pallas_call | solution.py:515
  30.4 0.1 collective-permute-start.9
  30.5 4.0 %collective-permute-start.6 = (bf16[192,128]{1,0:T(8,128)(2,1)S(1)}, bf16[192,128]{1,0:T(8,128)(2,1)S(1)}, u32[]{:S(2)}, u32[]{:S(2)}) collective-permute-start(bf16[192,128]{1,0:T(8,128)(2,1)S(1)} %shard_map.81.refs_0_.refs_1_), channel_id=1, source_target_pairs={{0,2},{1,3},{2,0},{3,1},{4,6},{5,7},{6,4},{7,5},{8,10},{9,11},{10,... | collective-permute-start | bytes 147464 | tf_op jit(solution)/shard_map/ppermute | solution.py:587
  34.5 0.5 collective-permute-start.7
  35.0 1.0 %collective-permute-start.8 = (bf16[192,128]{1,0:T(8,128)(2,1)S(1)}, bf16[192,128]{1,0:T(8,128)(2,1)S(1)}, u32[]{:S(2)}, u32[]{:S(2)}) collective-permute-start(bf16[192,128]{1,0:T(8,128)(2,1)S(1)} %shard_map.81.refs_0_.refs_1_), channel_id=1, source_target_pairs={{0,18},{1,19},{2,16},{3,17},{4,22},{5,23},{6,20},{7,21},{8,26},{9,... | collective-permute-start | bytes 147464 | tf_op jit(solution)/shard_map/ppermute | solution.py:587
  36.0 0.8 %collective-permute-done.6.refs_2_ = bf16[192,128]{1,0:T(8,128)(2,1)S(1)} collective-permute-done((bf16[192,128]{1,0:T(8,128)(2,1)S(1)}, bf16[192,128]{1,0:T(8,128)(2,1)S(1)}, u32[]{:S(2)}, u32[]{:S(2)}) %collective-permute-start.6) | collective-permute-done | bytes 49184 | tf_op jit(solution)/shard_map/ppermute | solution.py:587
  36.8 2.0 %collective-permute-done.7.refs_3_ = bf16[192,128]{1,0:T(8,128)(2,1)S(1)} collective-permute-done((bf16[192,128]{1,0:T(8,128)(2,1)S(1)}, bf16[192,128]{1,0:T(8,128)(2,1)S(1)}, u32[]{:S(2)}, u32[]{:S(2)}) %collective-permute-start.7) | collective-permute-done | bytes 49184 | tf_op jit(solution)/shard_map/ppermute | solution.py:587
  38.8 1.2 %collective-permute-done.8.refs_4_ = bf16[192,128]{1,0:T(8,128)(2,1)S(1)} collective-permute-done((bf16[192,128]{1,0:T(8,128)(2,1)S(1)}, bf16[192,128]{1,0:T(8,128)(2,1)S(1)}, u32[]{:S(2)}, u32[]{:S(2)}) %collective-permute-start.8) | collective-permute-done | bytes 49184 | tf_op jit(solution)/shard_map/ppermute | solution.py:587
  40.1 1.7 %collective-permute-start.11 = (bf16[192,128]{1,0:T(8,128)(2,1)S(1)}, bf16[192,128]{1,0:T(8,128)(2,1)S(1)}, u32[]{:S(2)}, u32[]{:S(2)}) collective-permute-start(bf16[192,128]{1,0:T(8,128)(2,1)S(1)} %shard_map.83.refs_0_.refs_1_), channel_id=1, source_target_pairs={{0,4},{1,5},{2,6},{3,7},{4,0},{5,1},{6,2},{7,3},{8,12},{9,13},{10,... | collective-permute-start | bytes 147464 | tf_op jit(solution)/shard_map/ppermute | solution.py:587
  41.7 2.2 %collective-permute-start.12 = (bf16[192,128]{1,0:T(8,128)(2,1)S(1)}, bf16[192,128]{1,0:T(8,128)(2,1)S(1)}, u32[]{:S(2)}, u32[]{:S(2)}) collective-permute-start(bf16[192,128]{1,0:T(8,128)(2,1)S(1)} %shard_map.83.refs_0_.refs_1_), channel_id=1, source_target_pairs={{0,8},{1,9},{2,10},{3,11},{4,12},{5,13},{6,14},{7,15},{8,0},{9,1},... | collective-permute-start | bytes 147464 | tf_op jit(solution)/shard_map/ppermute | solution.py:587
  44.0 0.5 collective-permute-start.13
  44.5 0.0 collective-permute-done.9.refs_1_.refs_4_
  44.5 0.1 shard_map.84.refs_1_
  44.6 1.3 %collective-permute-start.15 = (bf16[4,64,320]{2,1,0:T(8,128)(2,1)S(1)}, bf16[4,64,320]{2,1,0:T(8,128)(2,1)S(1)}, u32[]{:S(2)}, u32[]{:S(2)}) collective-permute-start(bf16[4,64,320]{2,1,0:T(8,128)(2,1)S(1)} %shard_map.84.refs_1_), channel_id=1, source_target_pairs={{2,0},{3,1},{4,2},{5,3},{6,4},{7,5},{8,6},{9,7},{10,8},{11,9},{12,... | collective-permute-start | bytes 491528 | tf_op jit(solution)/shard_map/ppermute | solution.py:531
  45.9 0.0 collective-permute-done.10.refs_3_.refs_4_
  45.9 3.9 %shard_map.85 = (bf16[24,4,32,64]{3,2,1,0:T(8,128)(2,1)}, f32[8,128]{1,0:T(8,128)S(1)}) custom-call(bf16[192,128]{1,0:T(8,128)(2,1)S(1)} %shard_map.83.refs_0_.refs_1_, bf16[4,64,320]{2,1,0:T(8,128)(2,1)S(1)} %shard_map.84.refs_1_, f32[2,24,80,128]{3,2,1,0:T(8,128)S(1)} %get-tuple-element.35.refs_0_.refs_2_, ...), custom_call_target="tpu_custom_call" | custom-call | flops 4369999872 | bytes 14060000 | tf_op jit(solution)/shard_map/pallas_call | solution.py:515
  49.8 0.0 collective-permute-done.11.refs_2_
  49.8 0.0 collective-permute-done.12.refs_3_
  49.8 0.5 collective-permute-done.13.refs_4_
  50.4 0.1 collective-permute-start.14
  50.4 1.9 %shard_map.87 = (bf16[4,64,320]{2,1,0:T(8,128)(2,1)}, f32[8,128]{1,0:T(8,128)S(1)}) custom-call(f32[192,128]{1,0:T(8,128)S(1)} %shard_map.86.refs_0_.refs_1_, f32[4,24,64,128]{3,2,1,0:T(8,128)S(1)} %get-tuple-element.49.refs_1_, f32[4,176,512]{2,1,0:T(8,128)S(1)} %get-tuple-element.50.refs_2_, f32[4,176,512]{2,1,0:T(8,128)S(1)} %get-tuple-element.51.refs_3_), custom_call_target="tpu_custom_call" | custom-call | flops 2184999936 | bytes 7030000 | tf_op jit(solution)/shard_map/pallas_call | solution.py:515
  52.4 0.0 collective-permute-done.14.refs_2_
  52.4 0.0 collective-permute-done.15.refs_5_
  52.4 1.1 %shard_map.88 = (f32[3,3,3,32,40]{4,3,2,1,0:T(8,128)}, bf16[4,64,320]{2,1,0:T(8,128)(2,1)}) custom-call(f32[8,128]{1,0:T(8,128)S(1)} %get-tuple-element.52.refs_0_, f32[192,128]{1,0:T(8,128)S(1)} %shard_map.86.refs_0_.refs_1_, f32[192,128]{1,0:T(8,128)S(1)} %collective-permute-done.14.refs_2_, bf16[4,64,320]{2,1,0:T(8,128)(2,1)S(1)} %get-tuple-element.42.refs_0_.refs_3_, ...), custom_call_target="tpu_custom_call" | custom-call | flops 1150000000 | bytes 3700000 | tf_op jit(solution)/shard_map/pallas_call | solution.py:515
  (3 shorter events, 0.1 us)
Async XLA Ops:
  0.6 9.3 %collective-permute-start.1 = (bf16[4,64,320]{2,1,0:T(8,128)(2,1)}, bf16[4,64,320]{2,1,0:T(8,128)(2,1)S(1)}, u32[]{:S(2)}, u32[]{:S(2)}) collective-permute-start(bf16[4,64,320]{2,1,0:T(8,128)(2,1)} %refs_2_.1), channel_id=1, source_target_pairs={{0,2},{1,3},{2,4},{3,5},{4,6},{5,7},{6,8},{7,9},{8,10},{9,11},{10,... | collective-permute-start | bytes 491528 | tf_op jit(solution)/shard_map/ppermute | solution.py:531
  5.5 0.9 %copy-start = (bf16[4,64,320]{2,1,0:T(8,128)(2,1)S(1)}, bf16[4,64,320]{2,1,0:T(8,128)(2,1)}, u32[]{:S(2)}) copy-start(bf16[4,64,320]{2,1,0:T(8,128)(2,1)} %refs_2_.1) | copy-start | bytes 491524
  6.5 1.1 %copy-start.2 = (bf16[24,4,64,32]{2,3,1,0:T(8,128)(2,1)S(1)}, bf16[24,4,64,32]{2,3,1,0:T(8,128)(2,1)}, u32[]{:S(2)}) copy-start(bf16[24,4,64,32]{2,3,1,0:T(8,128)(2,1)} %param.7) | copy-start | bytes 1179652
  7.6 0.9 %copy-start.4 = (bf16[4,64,320]{2,1,0:T(8,128)(2,1)S(1)}, bf16[4,64,320]{2,1,0:T(8,128)(2,1)}, u32[]{:S(2)}) copy-start(bf16[4,64,320]{2,1,0:T(8,128)(2,1)} %refs_1_.3) | copy-start | bytes 491524
  8.5 1.5 %copy-start.1 = (bf16[4,64,320]{2,1,0:T(8,128)(2,1)S(1)}, bf16[4,64,320]{2,1,0:T(8,128)(2,1)}, u32[]{:S(2)}) copy-start(bf16[4,64,320]{2,1,0:T(8,128)(2,1)} %refs_2_.1) | copy-start | bytes 491524
  10.0 3.2 %collective-permute-start.3 = (bf16[4,64,320]{2,1,0:T(8,128)(2,1)S(1)}, bf16[4,64,320]{2,1,0:T(8,128)(2,1)S(1)}, u32[]{:S(2)}, u32[]{:S(2)}) collective-permute-start(bf16[4,64,320]{2,1,0:T(8,128)(2,1)S(1)} %get-tuple-element.34), channel_id=1, source_target_pairs={{0,1},{1,0},{2,3},{3,2},{4,5},{5,4},{6,7},{7,6},{8,9},{9,8},{10,11... | collective-permute-start | bytes 491528 | tf_op jit(solution)/shard_map/ppermute | solution.py:587
  10.1 1.5 %collective-permute-start = (bf16[32,320]{1,0:T(8,128)(2,1)S(1)}, bf16[32,320]{1,0:T(8,128)(2,1)S(1)}, u32[]{:S(2)}, u32[]{:S(2)}) collective-permute-start(bf16[32,320]{1,0:T(8,128)(2,1)S(1)} %get-tuple-element.30), channel_id=1, source_target_pairs={{0,1},{1,0},{2,3},{3,2},{4,5},{5,4},{6,7},{7,6},{8,9},{9,8},{10,11... | collective-permute-start | bytes 61448 | tf_op jit(solution)/shard_map/ppermute | solution.py:587
  10.6 1.0 %collective-permute-start.2 = (bf16[32,320]{1,0:T(8,128)(2,1)S(1)}, bf16[32,320]{1,0:T(8,128)(2,1)S(1)}, u32[]{:S(2)}, u32[]{:S(2)}) collective-permute-start(bf16[32,320]{1,0:T(8,128)(2,1)S(1)} %get-tuple-element.32), channel_id=1, source_target_pairs={{1,2},{3,4},{5,6},{7,8},{9,10},{11,12},{13,14},{2,1},{4,3},{6,5},{... | collective-permute-start | bytes 61448 | tf_op jit(solution)/shard_map/ppermute | solution.py:615
  11.7 4.9 %collective-permute-start.4 = (bf16[6,80,128]{2,1,0:T(8,128)(2,1)S(1)}, bf16[6,80,128]{2,1,0:T(8,128)(2,1)S(1)}, u32[]{:S(2)}, u32[]{:S(2)}) collective-permute-start(bf16[6,80,128]{2,1,0:T(8,128)(2,1)S(1)} %shard_map.77.refs_0_), channel_id=1, source_target_pairs={{0,16},{16,0},{1,17},{17,1},{2,18},{18,2},{3,19},{19,3},{4,20},{20... | collective-permute-start | bytes 368648 | tf_op jit(solution)/shard_map/ppermute | solution.py:542
  16.6 9.1 %copy-start.3 = (bf16[3,3,3,40,32]{3,4,2,1,0:T(8,128)(2,1)S(1)}, bf16[3,3,3,40,32]{3,4,2,1,0:T(8,128)(2,1)}, u32[]{:S(2)}) copy-start(bf16[3,3,3,40,32]{3,4,2,1,0:T(8,128)(2,1)} %param.6) | copy-start | bytes 207364
  20.1 6.4 %collective-permute-start.5 = (f32[192,128]{1,0:T(8,128)S(1)}, f32[192,128]{1,0:T(8,128)S(1)}, u32[]{:S(2)}, u32[]{:S(2)}) collective-permute-start(f32[192,128]{1,0:T(8,128)S(1)} %get-tuple-element.39), channel_id=1, source_target_pairs={{0,1},{1,0},{2,3},{3,2},{4,5},{5,4},{6,7},{7,6},{8,9},{9,8},{10,11... | collective-permute-start | bytes 294920 | tf_op jit(solution)/shard_map/ppermute | solution.py:587
  24.2 21.7 %collective-permute-start.10 = (bf16[960,128]{1,0:T(8,128)(2,1)S(1)}, bf16[960,128]{1,0:T(8,128)(2,1)S(1)}, u32[]{:S(2)}, u32[]{:S(2)}) collective-permute-start(bf16[960,128]{1,0:T(8,128)(2,1)S(1)} %get-tuple-element.45), channel_id=1, source_target_pairs={{0,16},{16,0},{1,17},{17,1},{2,18},{18,2},{3,19},{19,3},{4,20},{20... | collective-permute-start | bytes 737288 | tf_op jit(solution)/shard_map/ppermute | solution.py:542
  30.4 14.1 %collective-permute-start.9 = (bf16[4,64,320]{2,1,0:T(8,128)(2,1)S(1)}, bf16[4,64,320]{2,1,0:T(8,128)(2,1)S(1)}, u32[]{:S(2)}, u32[]{:S(2)}) collective-permute-start(bf16[4,64,320]{2,1,0:T(8,128)(2,1)S(1)} %get-tuple-element.43), channel_id=1, source_target_pairs={{0,1},{1,0},{2,3},{3,2},{4,5},{5,4},{6,7},{7,6},{8,9},{9,8},{10,11... | collective-permute-start | bytes 491528 | tf_op jit(solution)/shard_map/ppermute | solution.py:587
  30.5 6.4 %collective-permute-start.6 = (bf16[192,128]{1,0:T(8,128)(2,1)S(1)}, bf16[192,128]{1,0:T(8,128)(2,1)S(1)}, u32[]{:S(2)}, u32[]{:S(2)}) collective-permute-start(bf16[192,128]{1,0:T(8,128)(2,1)S(1)} %shard_map.81.refs_0_.refs_1_), channel_id=1, source_target_pairs={{0,2},{1,3},{2,0},{3,1},{4,6},{5,7},{6,4},{7,5},{8,10},{9,11},{10,... | collective-permute-start | bytes 147464 | tf_op jit(solution)/shard_map/ppermute | solution.py:587
  34.5 4.3 %collective-permute-start.7 = (bf16[192,128]{1,0:T(8,128)(2,1)S(1)}, bf16[192,128]{1,0:T(8,128)(2,1)S(1)}, u32[]{:S(2)}, u32[]{:S(2)}) collective-permute-start(bf16[192,128]{1,0:T(8,128)(2,1)S(1)} %shard_map.81.refs_0_.refs_1_), channel_id=1, source_target_pairs={{0,16},{1,17},{2,18},{3,19},{4,20},{5,21},{6,22},{7,23},{8,24},{9,... | collective-permute-start | bytes 147464 | tf_op jit(solution)/shard_map/ppermute | solution.py:587
  35.0 5.0 %collective-permute-start.8 = (bf16[192,128]{1,0:T(8,128)(2,1)S(1)}, bf16[192,128]{1,0:T(8,128)(2,1)S(1)}, u32[]{:S(2)}, u32[]{:S(2)}) collective-permute-start(bf16[192,128]{1,0:T(8,128)(2,1)S(1)} %shard_map.81.refs_0_.refs_1_), channel_id=1, source_target_pairs={{0,18},{1,19},{2,16},{3,17},{4,22},{5,23},{6,20},{7,21},{8,26},{9,... | collective-permute-start | bytes 147464 | tf_op jit(solution)/shard_map/ppermute | solution.py:587
  40.1 9.8 %collective-permute-start.11 = (bf16[192,128]{1,0:T(8,128)(2,1)S(1)}, bf16[192,128]{1,0:T(8,128)(2,1)S(1)}, u32[]{:S(2)}, u32[]{:S(2)}) collective-permute-start(bf16[192,128]{1,0:T(8,128)(2,1)S(1)} %shard_map.83.refs_0_.refs_1_), channel_id=1, source_target_pairs={{0,4},{1,5},{2,6},{3,7},{4,0},{5,1},{6,2},{7,3},{8,12},{9,13},{10,... | collective-permute-start | bytes 147464 | tf_op jit(solution)/shard_map/ppermute | solution.py:587
  41.7 8.1 %collective-permute-start.12 = (bf16[192,128]{1,0:T(8,128)(2,1)S(1)}, bf16[192,128]{1,0:T(8,128)(2,1)S(1)}, u32[]{:S(2)}, u32[]{:S(2)}) collective-permute-start(bf16[192,128]{1,0:T(8,128)(2,1)S(1)} %shard_map.83.refs_0_.refs_1_), channel_id=1, source_target_pairs={{0,8},{1,9},{2,10},{3,11},{4,12},{5,13},{6,14},{7,15},{8,0},{9,1},... | collective-permute-start | bytes 147464 | tf_op jit(solution)/shard_map/ppermute | solution.py:587
  44.0 6.4 %collective-permute-start.13 = (bf16[192,128]{1,0:T(8,128)(2,1)S(1)}, bf16[192,128]{1,0:T(8,128)(2,1)S(1)}, u32[]{:S(2)}, u32[]{:S(2)}) collective-permute-start(bf16[192,128]{1,0:T(8,128)(2,1)S(1)} %shard_map.83.refs_0_.refs_1_), channel_id=1, source_target_pairs={{0,12},{1,13},{2,14},{3,15},{4,8},{5,9},{6,10},{7,11},{8,4},{9,5},... | collective-permute-start | bytes 147464 | tf_op jit(solution)/shard_map/ppermute | solution.py:587
  44.6 7.8 %collective-permute-start.15 = (bf16[4,64,320]{2,1,0:T(8,128)(2,1)S(1)}, bf16[4,64,320]{2,1,0:T(8,128)(2,1)S(1)}, u32[]{:S(2)}, u32[]{:S(2)}) collective-permute-start(bf16[4,64,320]{2,1,0:T(8,128)(2,1)S(1)} %shard_map.84.refs_1_), channel_id=1, source_target_pairs={{2,0},{3,1},{4,2},{5,3},{6,4},{7,5},{8,6},{9,7},{10,8},{11,9},{12,... | collective-permute-start | bytes 491528 | tf_op jit(solution)/shard_map/ppermute | solution.py:531
  50.4 2.0 %collective-permute-start.14 = (f32[192,128]{1,0:T(8,128)S(1)}, f32[192,128]{1,0:T(8,128)S(1)}, u32[]{:S(2)}, u32[]{:S(2)}) collective-permute-start(f32[192,128]{1,0:T(8,128)S(1)} %shard_map.86.refs_0_.refs_1_), channel_id=1, source_target_pairs={{0,1},{1,0},{2,3},{3,2},{4,5},{5,4},{6,7},{7,6},{8,9},{9,8},{10,11... | collective-permute-start | bytes 294920 | tf_op jit(solution)/shard_map/ppermute | solution.py:587
where the time goes:
time: 53.7 us; the launch traced here: 53.4 us
  starting transfers between devices  24.7 us (46%)
  Pallas kernels  18.1 us (34%)
  waiting for transfers between devices  6.92 us (13%)
  local copies, waits for them, and re-layouts  2.99 us (6%)
  between operations  0.77 us (1%)
    pallas_call x14, Pallas kernels, call(): pl.pallas_call(lambda *refs: kernel(*refs[skip:]), out_shape=[jax.ShapeDt...  18.1 us
    ppermute x11, starting transfers between devices, swap(): return lax.ppermute(block, ('row', 'col'), route)  14.8 us
    ppermute x2, starting transfers between devices, col_shift(): return lax.ppermute(block, 'col', route)  6.17 us
    ppermute x11, waiting for transfers between devices, swap(): return lax.ppermute(block, ('row', 'col'), route)  4.81 us
    ppermute x2, starting transfers between devices, halos(): got = lax.ppermute(pays[0], 'row', [(0, 1), (1, 0)])  3.05 us
    unnamed x10, local copies, waits for them, and re-layouts  2.99 us
    ppermute x2, waiting for transfers between devices, col_shift(): return lax.ppermute(block, 'col', route)  1.12 us
  transfers between devices with their start and end apart: 16, of which 7 were waited for; matrix products, arithmetic and copies ran while one was open for 0% of the time, Pallas kernels for 25%

commit v1 on v0

--- a/solution.py
+++ b/solution.py
@@ -68,8 +68,7 @@
             ).T
 
 
-def pass_kernel(own, got, end, out, end_out):
-    end_out[...] = end[...]
+def pass_kernel(own, got, out):
     out[...] = jnp.where(parity() == 0, own[...].astype(F32), got[...].astype(F32)).astype(BF16)
 
 
@@ -196,63 +195,88 @@
             pay[dd * total : (dd + 1) * total] = out.astype(BF16)
 
 
-def weight_kernel(masks, groups, vbuf, ctl, by_even, by_odd, top, bot, keep_out, give_out, ctsh, vt, buf, sums):
+def weight_kernel(
+    masks, groups, feat, vbuf, ctl, by_even, by_odd, top, bot, keep_out, give_out, ctsh, vt, buf, sums
+):
     disp, cols, width = ctl.shape
-    rows, feat = 2 * vbuf.shape[0], 32
-    per = 128 // feat
+    pairs, per, half = vbuf.shape[0], 128 // feat, disp // 2
     mtop, mbot = masks()
-    ctsh[0] = jnp.zeros(ctsh.shape[1:], BF16)
-    ctsh[disp + 1] = jnp.zeros(ctsh.shape[1:], BF16)
-    lane = lanes(top.shape[1:])
+    ctsh[0, 0] = jnp.zeros(ctsh.shape[2:], BF16)
+    ctsh[half, 1] = jnp.zeros(ctsh.shape[2:], BF16)
+    lane, lane_in, lane_one = lanes(top.shape[1:]), lanes((cols, 128)), lanes((1, 128))
+    shifts = (feat, 128 - feat)
     edges = [x[0:disp, 0:128] for x in end_columns(by_even, by_odd)]
-    for d in range(disp):
-        buf[d, PAD - 1 : PAD, 0:128] = edges[0][d : d + 1]
-        buf[d, PAD + cols : PAD + cols + 1, 0:128] = edges[1][d : d + 1]
-
-    def fill(q, _):
+    turned = [[pltpu.roll(x, shift, 1) for shift in shifts] for x in edges]
+    for q in range(disp // per):
         t = top[q].astype(F32) * mtop
         z = bot[q].astype(F32) * mbot
         for i in range(per):
             d = q * per + i
-            a = t if i == 0 else pltpu.roll(t, 128 - feat * i, 1)
-            y = z if i == 1 else pltpu.roll(z, (128 + feat - feat * i) % 128, 1)
-            buf[d, PAD : PAD + cols, 0:128] = ctl[d].astype(F32)
-            buf[d, :, 128:256] = jnp.where(lane < feat, a, jnp.where(lane < 2 * feat, y, 0.0))
+            rims = (
+                t if i == 0 else pltpu.roll(t, 128 - feat * i, 1),
+                z if i == per - 1 else pltpu.roll(z, feat * (per - 1 - i), 1),
+            )
+            inner = ctl[d].astype(F32)
+            for p, (rim, shift) in enumerate(zip(rims, shifts)):
+
+                def on_rim(x):
+                    return x < feat if p == 0 else x >= 128 - feat
+
+                at = slice(128 * p, 128 * (p + 1))
+                buf[d, PAD : PAD + cols, at] = jnp.where(
+                    on_rim(lane_in), rim[PAD : PAD + cols], pltpu.roll(inner, shift, 1)
+                )
+                for side, row in enumerate((PAD - 1, PAD + cols)):
+                    buf[d, row : row + 1, at] = jnp.where(
+                        on_rim(lane_one), rim[row : row + 1], turned[side][p][d : d + 1]
+                    )
             for e in range(3):
-                ctsh[d + 1, :, 256 * e : 256 * (e + 1)] = buf[
+                ctsh[(d + 1) // 2, (d + 1) % 2, :, 256 * e : 256 * (e + 1)] = buf[
                     d, PAD - 1 + e : PAD - 1 + e + cols
                 ].astype(BF16)
-        return 0
-
-    lax.fori_loop(0, disp // per, fill, 0, unroll=True)
-    step = 256 // cols
-    for q in range(disp // step):
-        for p in range(rows // 2):
-            v = vbuf[p, q * step : (q + 1) * step, PAD : PAD + cols].reshape(256, 128).astype(BF16)
-            vt[128 * p : 128 * (p + 1), 256 * q : 256 * (q + 1)] = v.T
-    keep = lanes((groups, 128))
+    none = jnp.zeros((cols, 128), F32)
+    for p in range(pairs):
+        for j in range(-1, half + 1):
+            block = [
+                vbuf[p, d, PAD : PAD + cols] if 0 <= d < disp and 0 <= j + half * o else none
+                for o, d in enumerate((j, j + half))
+            ]
+            if j == half:
+                block[1] = none
+            x = jnp.concatenate(block, axis=0).astype(BF16)
+            vt[p, :, 128 * (j + 1) : 128 * (j + 2)] = x.T
+    size = disp * cols
+    left = jnp.concatenate(
+        [
+            jnp.concatenate([vt[p, :, 128 * (2 - a) : 128 * (2 - a) + size] for p in range(pairs)], axis=1)
+            for a in range(3)
+        ],
+        axis=0,
+    )
+    right = jnp.concatenate(
+        [
+            jnp.concatenate(
+                [
+                    ctsh[(d + 1) // 2, (d + 1) % 2, :, 256 * e + 128 * p : 256 * e + 128 * (p + 1)]
+                    for e in range(3)
+                ],
+                axis=1,
+            )
+            for p in range(pairs)
+            for j in range(half)
+            for d in (j, j + half)
+        ],
+        axis=0,
+    )
+    full = dot(left, right)
+    keep = lanes((groups, 128)) < 3 * feat
     sums[...] = jnp.zeros(sums.shape, F32)
-
-    def taps(a, _):
+    for a in range(3):
         for e in range(3):
-            ct_block = ctsh[pl.ds(a, disp), :, 256 * e : 256 * (e + 1)].reshape(disp * cols, 256)
-            full = dot(vt[...], ct_block)
-            out = None
-            for h in range(rows):
-                x = full[SLOT * h : SLOT * h + groups, 0:128]
-                y = full[SLOT * h : SLOT * h + groups, 128:256]
-                if h == 0:
-                    term = jnp.where(keep < feat, y, pltpu.roll(x, feat, 1))
-                else:
-                    term = x if h == 1 else pltpu.roll(x, 128 - feat * (h - 1), 1)
-                    if h == rows - 1:
-                        term = jnp.where(keep < 2 * feat, term, pltpu.roll(y, feat, 1))
-                out = term if out is None else out + term
-            at = pl.multiple_of(a * 128 + groups * e, 8)
-            sums[pl.ds(at, groups)] = jnp.where(keep < 3 * feat, out, 0.0)
-        return 0
-
-    lax.fori_loop(0, 3, taps, 0)
+            block = full[128 * a : 128 * (a + 1), 128 * e : 128 * (e + 1)]
+            out = block[0:groups] + pltpu.roll(block[SLOT : SLOT + groups], 128 - feat, 1)
+            at = 128 * a + groups * e
+            sums[at : at + groups] = jnp.where(keep, out, 0.0)
     half = sums.shape[0] // 2
     is_even = parity() == 0
     low, high = sums[0:half], sums[half:]
@@ -261,26 +285,32 @@
 
 
 def right_kernel(ctsh, w2, fl, gv, rg0, rg1, rg2, acce, acco, both):
-    disp = ctsh.shape[0] - 2
+    disp = gv.shape[1]
     rows, cols, channels = rg0.shape
     wide = fl.shape[2]
     group_size = wide // SLOT
-    step = 512 // cols
-    low = lanes((512, 128)) < SLOT
+    step = disp // 4
+    low = lanes((step * cols, 128)) < SLOT
 
     def conv(q, _):
-        slabs = [ctsh[pl.ds(q * step + a, step)].reshape(512, ctsh.shape[2]) for a in range(3)]
-        acc = dot(jnp.concatenate(slabs, axis=1), w2[...])
-        g = acc.astype(BF16).astype(F32)
         for p in range(rows // 2):
-            x = g[:, 128 * p : 128 * (p + 1)]
-            r = pltpu.roll(x, SLOT, 1)
+            slabs = [
+                ctsh[pl.ds(q * step + s // 2, step), s % 2, :, 256 * e + 128 * p : 256 * e + 128 * (p + 1)]
+                for s in range(4)
+                for e in range(3)
+            ]
+            slabs = [x.reshape(step * cols, 128) for x in slabs]
+            acc = dot(jnp.concatenate(slabs, axis=1), w2[...]).astype(BF16).astype(F32)
             for o in range(2):
-                y = jnp.where(low, r, x) if o else jnp.where(low, x, r)
-                gv[2 * p + o, pl.ds(q * step, step)] = y.reshape(step, cols, 128)
+                x = acc[:, 128 * o : 128 * (o + 1)]
+                r = pltpu.roll(x, SLOT, 1)
+                for hh in range(2):
+                    y = jnp.where(low, r, x) if hh else jnp.where(low, x, r)
+                    for j in range(step):
+                        gv[2 * p + hh, 2 * (q * step + j) + o] = y[j * cols : (j + 1) * cols]
         return 0
 
-    lax.fori_loop(0, disp // step, conv, 0)
+    lax.fori_loop(0, 2, conv, 0)
     count = cols // 8
     back = acce.shape[1] - cols
     lead = back // 8
@@ -458,9 +488,6 @@
         def at_row(h):
             return pl.multiple_of((a * rows + h) * feat, feat)
 
-        def at_tap(row):
-            return pl.multiple_of(a * 3 * 256 + row, feat)
-
         for e in range(3):
             for h in range(rows):
                 for p in range(rows // 2):
@@ -471,19 +498,16 @@
                     if h == rows - 1 and p == rows // 2 - 1:
                         block = place_halo(block, wide(a, 2, e), groups, 0, lane_of)
                     turned[pl.ds(at_row(h), feat), lane : lane + 2 * SLOT] = block
-            for slot, six in enumerate((*range(1, rows + 1), 0, rows + 1)):
-                at = 256 * e + feat * slot
-                for p in range(rows // 2):
-                    back = [2 - (six - 2 * p - o) for o in range(2)]
-                    w2[pl.ds(at_tap(at), feat), 2 * SLOT * p : 2 * SLOT * (p + 1)] = beside(
-                        wide(2 - a, back[0], 2 - e), wide(2 - a, back[1], 2 - e)
-                    ).astype(BF16)
-            at = 256 * e + feat * (rows + 2)
-            size = 256 - feat * (rows + 2)
-            w2[pl.ds(at_tap(at), size)] = jnp.zeros((size, rows * SLOT), BF16)
         return 0
 
     lax.fori_loop(0, 3, build, 0)
+    for s in range(4):
+        for e in range(3):
+            for r in range(4):
+                for o in range(2):
+                    taps_of = [None if not 0 <= s - o <= 2 else wide(2 - s + o, 2 - r + i, 2 - e) for i in range(2)]
+                    at = 384 * s + 128 * e + feat * r
+                    w2[at : at + feat, 128 * o : 128 * (o + 1)] = beside(*taps_of).astype(BF16)
     depth, size = turned.shape[1], rows * feat
     for a in range(3):
         for i in range(depth // 128):
@@ -601,17 +625,8 @@
         ct,
         us=0.4,
     )
+    inner = range(1, n_col - 1, 2)
     by_even = swap(by_even, 1)
-    near, by_odd = call(
-        pass_kernel,
-        [((rows, cols, channels), BF16), ((count, channels), BF16)],
-        [],
-        right_features,
-        far,
-        by_odd,
-    )
-    near = swap(near, 1)
-    inner = range(1, n_col - 1, 2)
     by_odd = lax.ppermute(by_odd, "col", [(i, i + 1) for i in inner] + [(i + 1, i) for i in inner])
     row_pays = call(
         functools.partial(row_kernel, ends, rows),
@@ -622,6 +637,10 @@
         *rims,
     )
     top, bot = halos(row_pays)
+    (near,) = call(
+        pass_kernel, [((rows, cols, channels), BF16)], [], right_features, far, after=row_pays
+    )
+    near = swap(near, 1)
 
     band = 104 + cols + PAD
     spread_rows = 3 * rows * cols + rows * cols // 2 + 2 * count
@@ -644,26 +663,25 @@
         far,
         by_even,
         by_odd,
-        after=row_pays,
         us=2.3,
     )
     vtop, vbot = halos(volume_rows)
 
     keep, give, ctsh = call(
-        functools.partial(weight_kernel, masks, groups),
-        [((3 * 64, 128), F32), ((3 * 64, 128), F32), ((disp + 2, cols, 3 * 256), BF16)],
-        [
-            pltpu.VMEM((rows * SLOT, disp * cols), BF16),
+        functools.partial(weight_kernel, masks, groups, feat),
+        [((3 * 64, 128), F32), ((3 * 64, 128), F32), ((disp // 2 + 1, 2, cols, 3 * 256), BF16)],
+        [
+            pltpu.VMEM((rows // 2, 128, (disp // 2 + 2) * 128), BF16),
             pltpu.VMEM((disp, total, 256), F32),
             pltpu.VMEM((3 * 128, 128), F32),
         ],
         vbuf, ctl, by_even, by_odd, top, bot,
-        us=3.4,
+        us=2.6,
     )
     got = swap(give, 1)
     w2, wc = call(
         taps_kernel,
-        [((9 * 256, rows * SLOT), BF16), ((4 * 3 * rows * SLOT, 2 * rows * feat), BF16)],
+        [((12 * 128, 2 * 128), BF16), ((4 * 3 * rows * SLOT, 2 * rows * feat), BF16)],
         [pltpu.VMEM((3 * rows * feat, 3 * rows * SLOT), F32)],
         conv_weight.transpose(0, 1, 2, 4, 3),
         after=[keep],
@@ -685,7 +703,7 @@
         ],
         ctsh, w2, fl,
         after=[part],
-        us=3.8,
+        us=2.9,
     )
     rg1 = swap(rg1, 1)
     *middle, final = stages(n_row, n_col)
@@ -695,22 +713,6 @@
         (part,) = call(sum_kernel, [(part.shape, BF16)], [], *parts, after=order)
         order = []
     parts = [part] + [swap(part, m) for m in final]
-    (rg2,) = call(
-        combine_kernel, [((rows, cols, channels), BF16)], [], rg1, rg2, after=[part]
-    )
-    output, conv_done = call(
-        functools.partial(conv_kernel, masks, groups),
-        [((disp, rows, feat, cols), BF16)],
-        [
-            pltpu.VMEM((disp // 2 + 1, 2, cols, 3 * rows * SLOT), BF16),
-            pltpu.VMEM((rows // 2, disp, total, 128), F32),
-        ],
-        vbuf, vtop, vbot, wc,
-        after=[part, rg2],
-        token=True,
-        us=3.8,
-    )
-    (part,) = call(sum_kernel, [(part.shape, F32)], [], *parts, after=[conv_done])
     lg, left_done = call(
         left_kernel,
         [((rows, cols, channels), BF16)],
@@ -720,6 +722,22 @@
         token=True,
         us=1.9,
     )
+    (rg2,) = call(
+        combine_kernel, [((rows, cols, channels), BF16)], [], rg1, rg2, after=[left_done]
+    )
+    (part,) = call(sum_kernel, [(part.shape, F32)], [], *parts, after=[left_done])
+    output, conv_done = call(
+        functools.partial(conv_kernel, masks, groups),
+        [((disp, rows, feat, cols), BF16)],
+        [
+            pltpu.VMEM((disp // 2 + 1, 2, cols, 3 * rows * SLOT), BF16),
+            pltpu.VMEM((rows // 2, disp, total, 128), F32),
+        ],
+        vbuf, vtop, vbot, wc,
+        after=[part, rg2],
+        token=True,
+        us=3.9,
+    )
     rg2 = col_shift(rg2, -2)
     cells = disp * rows * n_row * cols * n_col
     weight_grad, right_grad = call(
@@ -727,7 +745,7 @@
         [((3, 3, 3, feat, groups), F32), ((rows, cols, channels), BF16)],
         [],
         part, swap(part, 1), rg0, rg1, rg2,
-        after=[left_done],
+        after=[conv_done],
         us=1.0,
     )
     return (

time: 53.7 us -> 53.9 us (level)
  waiting for transfers between devices: 6.92 us -> 11.3 us
  Pallas kernels: 18.1 us -> 15.8 us
  starting transfers between devices: 24.7 us -> 22.7 us
    ppermute x2, waiting for transfers between devices: 1.12 us -> 3.94 us  [col_shift(): return lax.ppermute(block, 'col', route)]
    pallas_call x14, Pallas kernels: 18.1 us -> 15.8 us  [call(): pl.pallas_call(lambda *refs: kernel(*refs[skip:]), out_shape=[jax.ShapeDt...]
    ppermute x11, starting transfers between devices: 14.8 us -> 12.8 us  [swap(): return lax.ppermute(block, ('row', 'col'), route)]
    ppermute x11, waiting for transfers between devices: 4.81 us -> 5.98 us  [swap(): return lax.ppermute(block, ('row', 'col'), route)]
    unnamed x10 -> x12, local copies, waits for them, and re-layouts: 2.99 us -> 2.99 us
  transfers between devices with their start and end apart: 16 -> 16, of which waited for: 7 -> 7; matrix products, arithmetic and copies ran while one was open for 0% -> 0% of each run, Pallas kernels for 25% -> 24%
where the time goes in v1:
time: 53.9 us; the launch traced here: 53.7 us
  starting transfers between devices  22.7 us (42%)
  Pallas kernels  15.8 us (29%)
  waiting for transfers between devices  11.3 us (21%)
  local copies, waits for them, and re-layouts  2.99 us (6%)
  between operations  0.82 us (2%)
    pallas_call x14, Pallas kernels, call(): pl.pallas_call(lambda *refs: kernel(*refs[skip:]), out_shape=[jax.ShapeDt...  15.8 us
    ppermute x11, starting transfers between devices, swap(): return lax.ppermute(block, ('row', 'col'), route)  12.8 us
    ppermute x2, starting transfers between devices, col_shift(): return lax.ppermute(block, 'col', route)  6.17 us
    ppermute x11, waiting for transfers between devices, swap(): return lax.ppermute(block, ('row', 'col'), route)  5.98 us
    ppermute x2, waiting for transfers between devices, col_shift(): return lax.ppermute(block, 'col', route)  3.94 us
    ppermute x2, starting transfers between devices, halos(): got = lax.ppermute(pays[0], 'row', [(0, 1), (1, 0)])  3.05 us
    unnamed x12, local copies, waits for them, and re-layouts  2.99 us
    ppermute x2, waiting for transfers between devices, halos(): got = lax.ppermute(pays[0], 'row', [(0, 1), (1, 0)])  1.41 us
  transfers between devices with their start and end apart: 16, of which 7 were waited for; matrix products, arithmetic and copies ran while one was open for 0% of the time, Pallas kernels for 24%

profile of v1, /device:TPU:0, one launch (start us, length us, event | category | flops | bytes accessed | tf_op | source)
XLA Modules:
  0.0 53.7 jit_solution(4416679343861126162)
XLA Ops:
  0.6 4.9 %collective-permute-start.2 = (bf16[4,64,320]{2,1,0:T(8,128)(2,1)}, bf16[4,64,320]{2,1,0:T(8,128)(2,1)S(1)}, u32[]{:S(2)}, u32[]{:S(2)}) collective-permute-start(bf16[4,64,320]{2,1,0:T(8,128)(2,1)} %refs_1_.5), channel_id=1, source_target_pairs={{0,2},{1,3},{2,4},{3,5},{4,6},{5,7},{6,8},{7,9},{8,10},{9,11},{10,... | collective-permute-start | bytes 491528 | tf_op jit(solution)/shard_map/ppermute | solution.py:555
  5.5 0.0 copy-start
  5.5 0.9 %copy-done = bf16[4,64,320]{2,1,0:T(8,128)(2,1)S(1)} copy-done((bf16[4,64,320]{2,1,0:T(8,128)(2,1)S(1)}, bf16[4,64,320]{2,1,0:T(8,128)(2,1)}, u32[]{:S(2)}) %copy-start) | copy-done | bytes 163864
  6.5 0.0 copy-start.2
  6.5 1.1 %copy-done.2 = bf16[24,4,64,32]{2,3,1,0:T(8,128)(2,1)S(1)} copy-done((bf16[24,4,64,32]{2,3,1,0:T(8,128)(2,1)S(1)}, bf16[24,4,64,32]{2,3,1,0:T(8,128)(2,1)}, u32[]{:S(2)}) %copy-start.2) | copy-done | bytes 393240
  7.6 0.0 copy-start.4
  7.6 0.9 %copy-done.4 = bf16[4,64,320]{2,1,0:T(8,128)(2,1)S(1)} copy-done((bf16[4,64,320]{2,1,0:T(8,128)(2,1)S(1)}, bf16[4,64,320]{2,1,0:T(8,128)(2,1)}, u32[]{:S(2)}) %copy-start.4) | copy-done | bytes 163864
  8.5 0.0 copy-start.1
  8.5 0.0 copy-start.5
  8.5 0.3 shard_map.75
  8.9 0.1 collective-permute-start
  8.9 0.7 %collective-permute-start.1 = (bf16[32,320]{1,0:T(8,128)(2,1)S(1)}, bf16[32,320]{1,0:T(8,128)(2,1)S(1)}, u32[]{:S(2)}, u32[]{:S(2)}) collective-permute-start(bf16[32,320]{1,0:T(8,128)(2,1)S(1)} %get-tuple-element.29), channel_id=1, source_target_pairs={{1,2},{3,4},{5,6},{7,8},{9,10},{11,12},{13,14},{2,1},{4,3},{6,5},{... | collective-permute-start | bytes 61448 | tf_op jit(solution)/shard_map/ppermute | solution.py:630
  9.6 0.5 collective-permute-done.refs_0_.refs_4_.refs_2_
  10.1 0.0 collective-permute-done.1.refs_1_.refs_5_.refs_3_
  10.1 0.1 shard_map.76.refs_0_
  10.2 0.0 collective-permute-done.2.refs_2_.refs_3_
  10.2 0.0 copy-done.1
  10.2 0.1 shard_map.77
  10.3 4.5 %collective-permute-start.3 = (bf16[4,64,320]{2,1,0:T(8,128)(2,1)S(1)}, bf16[4,64,320]{2,1,0:T(8,128)(2,1)S(1)}, u32[]{:S(2)}, u32[]{:S(2)}) collective-permute-start(bf16[4,64,320]{2,1,0:T(8,128)(2,1)S(1)} %shard_map.77), channel_id=1, source_target_pairs={{0,1},{1,0},{2,3},{3,2},{4,5},{5,4},{6,7},{7,6},{8,9},{9,8},{10,11... | collective-permute-start | bytes 491528 | tf_op jit(solution)/shard_map/ppermute | solution.py:611
  14.8 1.5 %collective-permute-start.4 = (bf16[6,80,128]{2,1,0:T(8,128)(2,1)S(1)}, bf16[6,80,128]{2,1,0:T(8,128)(2,1)S(1)}, u32[]{:S(2)}, u32[]{:S(2)}) collective-permute-start(bf16[6,80,128]{2,1,0:T(8,128)(2,1)S(1)} %shard_map.76.refs_0_), channel_id=1, source_target_pairs={{0,16},{16,0},{1,17},{17,1},{2,18},{18,2},{3,19},{19,3},{4,20},{20... | collective-permute-start | bytes 368648 | tf_op jit(solution)/shard_map/ppermute | solution.py:566
  16.3 0.0 collective-permute-done.3.refs_2_
  16.3 0.0 copy-done.5
  16.3 2.4 %shard_map.78 = (f32[2,24,80,128]{3,2,1,0:T(8,128)S(1)}, f32[4,80,512]{2,1,0:T(8,128)S(1)}, f32[4,176,512]{2,1,0:T(8,128)S(1)}, f32[4,176,512]{2,1,0:T(8,128)S(1)}, bf16[960,128]{1,0:T(8,128)(2,1)S(1)}) custom-call(bf16[4,64,320]{2,1,0:T(8,128)(2,1)S(1)} %copy-done.5, bf16[4,64,320]{2,1,0:T(8,128)(2,1)S(1)} %copy-done.1, ...), custom_call_target="tpu_custom_call" | custom-call | flops 2644999936 | bytes 8510000 | tf_op jit(solution)/shard_map/pallas_call | solution.py:539
  18.7 1.4 %collective-permute-done.4.refs_4_.refs_5_ = bf16[6,80,128]{2,1,0:T(8,128)(2,1)S(1)} collective-permute-done((bf16[6,80,128]{2,1,0:T(8,128)(2,1)S(1)}, bf16[6,80,128]{2,1,0:T(8,128)(2,1)S(1)}, u32[]{:S(2)}, u32[]{:S(2)}) %collective-permute-start.4) | collective-permute-done | bytes 122912 | tf_op jit(solution)/shard_map/ppermute | solution.py:566
  20.1 0.0 copy-start.3
  20.1 2.0 %shard_map.79 = (f32[192,128]{1,0:T(8,128)S(1)}, f32[192,128]{1,0:T(8,128)S(1)}, bf16[13,2,64,768]{3,2,1,0:T(8,128)(2,1)S(1)}) custom-call(f32[2,24,80,128]{3,2,1,0:T(8,128)S(1)} %get-tuple-element.31.refs_0_.refs_2_, bf16[24,64,128]{2,1,0:T(8,128)(2,1)S(1)} %get-tuple-element.32.refs_1_, bf16[32,320]{1,0:T(8,128)(2,1)S(1)} %collective-permute-done.refs_0_.refs_4_.refs_2_, ...), custom_call_target="tpu_custom_call" | custom-call | flops 2990000128 | bytes 9620000 | tf_op jit(solution)/shard_map/pallas_call | solution.py:539
  22.2 0.1 collective-permute-start.5
  22.2 1.6 %collective-permute-start.13 = (bf16[960,128]{1,0:T(8,128)(2,1)S(1)}, bf16[960,128]{1,0:T(8,128)(2,1)S(1)}, u32[]{:S(2)}, u32[]{:S(2)}) collective-permute-start(bf16[960,128]{1,0:T(8,128)(2,1)S(1)} %get-tuple-element.45), channel_id=1, source_target_pairs={{0,16},{16,0},{1,17},{17,1},{2,18},{18,2},{3,19},{19,3},{4,20},{20... | collective-permute-start | bytes 737288 | tf_op jit(solution)/shard_map/ppermute | solution.py:566
  23.8 0.0 copy-done.3
  23.8 0.8 %shard_map.80 = (bf16[1536,256]{1,0:T(8,128)(2,1)S(1)}, bf16[3072,256]{1,0:T(8,128)(2,1)S(1)}) custom-call(f32[192,128]{1,0:T(8,128)S(1)} %get-tuple-element.33.refs_0_.refs_1_, bf16[3,3,3,32,40]{4,3,2,1,0:T(8,128)(2,1)S(1)} %bitcast.5), custom_call_target="tpu_custom_call" | custom-call | flops 920000000 | bytes 2960000 | tf_op jit(solution)/shard_map/pallas_call | solution.py:539
  24.6 0.0 collective-permute-done.5.refs_2_
  24.7 2.5 %collective-permute-start.6 = (bf16[192,128]{1,0:T(8,128)(2,1)S(1)}, bf16[192,128]{1,0:T(8,128)(2,1)S(1)}, u32[]{:S(2)}, u32[]{:S(2)}) collective-permute-start(bf16[192,128]{1,0:T(8,128)(2,1)S(1)} %shard_map.81.refs_0_.refs_1_), channel_id=1, source_target_pairs={{0,2},{1,3},{2,0},{3,1},{4,6},{5,7},{6,4},{7,5},{8,10},{9,11},{10,... | collective-permute-start | bytes 147464 | tf_op jit(solution)/shard_map/ppermute | solution.py:611
  27.1 0.5 %collective-permute-start.7 = (bf16[192,128]{1,0:T(8,128)(2,1)S(1)}, bf16[192,128]{1,0:T(8,128)(2,1)S(1)}, u32[]{:S(2)}, u32[]{:S(2)}) collective-permute-start(bf16[192,128]{1,0:T(8,128)(2,1)S(1)} %shard_map.81.refs_0_.refs_1_), channel_id=1, source_target_pairs={{0,16},{1,17},{2,18},{3,19},{4,20},{5,21},{6,22},{7,23},{8,24},{9,... | collective-permute-start | bytes 147464 | tf_op jit(solution)/shard_map/ppermute | solution.py:611
  27.7 1.0 %collective-permute-start.8 = (bf16[192,128]{1,0:T(8,128)(2,1)S(1)}, bf16[192,128]{1,0:T(8,128)(2,1)S(1)}, u32[]{:S(2)}, u32[]{:S(2)}) collective-permute-start(bf16[192,128]{1,0:T(8,128)(2,1)S(1)} %shard_map.81.refs_0_.refs_1_), channel_id=1, source_target_pairs={{0,18},{1,19},{2,16},{3,17},{4,22},{5,23},{6,20},{7,21},{8,26},{9,... | collective-permute-start | bytes 147464 | tf_op jit(solution)/shard_map/ppermute | solution.py:611
  28.7 3.0 %shard_map.82 = (f32[4,24,64,128]{3,2,1,0:T(8,128)S(1)}, bf16[4,64,320]{2,1,0:T(8,128)(2,1)S(1)}, bf16[4,64,320]{2,1,0:T(8,128)(2,1)S(1)}, bf16[4,32,320]{2,1,0:T(8,128)(2,1)S(1)}) custom-call(bf16[192,128]{1,0:T(8,128)(2,1)S(1)} %shard_map.81.refs_0_.refs_1_, bf16[13,2,64,768]{3,2,1,0:T(8,128)(2,1)S(1)} %get-tuple-element.36.refs_1_, ...), custom_call_target="tpu_custom_call" | custom-call | flops 3335000064 | bytes 10730000 | tf_op jit(solution)/shard_map/pallas_call | solution.py:539
  31.7 0.1 collective-permute-start.12
  31.8 0.0 collective-permute-done.6.refs_2_
  31.8 0.3 collective-permute-done.7.refs_3_
  32.1 2.5 %collective-permute-done.8.refs_4_ = bf16[192,128]{1,0:T(8,128)(2,1)S(1)} collective-permute-done((bf16[192,128]{1,0:T(8,128)(2,1)S(1)}, bf16[192,128]{1,0:T(8,128)(2,1)S(1)}, u32[]{:S(2)}, u32[]{:S(2)}) %collective-permute-start.8) | collective-permute-done | bytes 49184 | tf_op jit(solution)/shard_map/ppermute | solution.py:611
  34.6 2.7 %collective-permute-start.10 = (bf16[192,128]{1,0:T(8,128)(2,1)S(1)}, bf16[192,128]{1,0:T(8,128)(2,1)S(1)}, u32[]{:S(2)}, u32[]{:S(2)}) collective-permute-start(bf16[192,128]{1,0:T(8,128)(2,1)S(1)} %shard_map.83.refs_0_.refs_1_), channel_id=1, source_target_pairs={{0,8},{1,9},{2,10},{3,11},{4,12},{5,13},{6,14},{7,15},{8,0},{9,1},... | collective-permute-start | bytes 147464 | tf_op jit(solution)/shard_map/ppermute | solution.py:611
  37.3 1.3 %collective-permute-start.11 = (bf16[192,128]{1,0:T(8,128)(2,1)S(1)}, bf16[192,128]{1,0:T(8,128)(2,1)S(1)}, u32[]{:S(2)}, u32[]{:S(2)}) collective-permute-start(bf16[192,128]{1,0:T(8,128)(2,1)S(1)} %shard_map.83.refs_0_.refs_1_), channel_id=1, source_target_pairs={{0,12},{1,13},{2,14},{3,15},{4,8},{5,9},{6,10},{7,11},{8,4},{9,5},... | collective-permute-start | bytes 147464 | tf_op jit(solution)/shard_map/ppermute | solution.py:611
  38.6 0.0 collective-permute-start.9
  38.6 1.9 %shard_map.84 = (bf16[4,64,320]{2,1,0:T(8,128)(2,1)}, f32[8,128]{1,0:T(8,128)S(1)}) custom-call(bf16[192,128]{1,0:T(8,128)(2,1)S(1)} %shard_map.83.refs_0_.refs_1_, f32[4,24,64,128]{3,2,1,0:T(8,128)S(1)} %get-tuple-element.39.refs_1_, f32[4,176,512]{2,1,0:T(8,128)S(1)} %get-tuple-element.40.refs_2_, f32[4,176,512]{2,1,0:T(8,128)S(1)} %get-tuple-element.41.refs_3_), custom_call_target="tpu_custom_call" | custom-call | flops 2184999936 | bytes 7030000 | tf_op jit(solution)/shard_map/pallas_call | solution.py:539
  40.5 0.4 collective-permute-done.10.refs_3_
  40.9 2.3 %collective-permute-done.11.refs_4_ = bf16[192,128]{1,0:T(8,128)(2,1)S(1)} collective-permute-done((bf16[192,128]{1,0:T(8,128)(2,1)S(1)}, bf16[192,128]{1,0:T(8,128)(2,1)S(1)}, u32[]{:S(2)}, u32[]{:S(2)}) %collective-permute-start.11) | collective-permute-done | bytes 49184 | tf_op jit(solution)/shard_map/ppermute | solution.py:611
  43.2 0.0 collective-permute-done.9.refs_2_
  43.2 0.1 collective-permute-start.14
  43.3 0.0 collective-permute-done.12.refs_1_.refs_4_
  43.3 0.1 shard_map.86.refs_1_
  43.4 1.3 %collective-permute-start.15 = (bf16[4,64,320]{2,1,0:T(8,128)(2,1)S(1)}, bf16[4,64,320]{2,1,0:T(8,128)(2,1)S(1)}, u32[]{:S(2)}, u32[]{:S(2)}) collective-permute-start(bf16[4,64,320]{2,1,0:T(8,128)(2,1)S(1)} %shard_map.86.refs_1_), channel_id=1, source_target_pairs={{2,0},{3,1},{4,2},{5,3},{6,4},{7,5},{8,6},{9,7},{10,8},{11,9},{12,... | collective-permute-start | bytes 491528 | tf_op jit(solution)/shard_map/ppermute | solution.py:555
  44.7 0.0 collective-permute-done.13.refs_3_.refs_4_
  44.7 3.9 %shard_map.87 = (bf16[24,4,32,64]{3,2,1,0:T(8,128)(2,1)}, f32[8,128]{1,0:T(8,128)S(1)}) custom-call(f32[192,128]{1,0:T(8,128)S(1)} %shard_map.85.refs_0_.refs_1_, bf16[4,64,320]{2,1,0:T(8,128)(2,1)S(1)} %shard_map.86.refs_1_, f32[2,24,80,128]{3,2,1,0:T(8,128)S(1)} %get-tuple-element.31.refs_0_.refs_2_, ...), custom_call_target="tpu_custom_call" | custom-call | flops 4485000192 | bytes 14430000 | tf_op jit(solution)/shard_map/pallas_call | solution.py:539
  48.7 0.0 collective-permute-done.14.refs_2_
  48.7 3.9 %collective-permute-done.15.refs_5_ = bf16[4,64,320]{2,1,0:T(8,128)(2,1)S(1)} collective-permute-done((bf16[4,64,320]{2,1,0:T(8,128)(2,1)S(1)}, bf16[4,64,320]{2,1,0:T(8,128)(2,1)S(1)}, u32[]{:S(2)}, u32[]{:S(2)}) %collective-permute-start.15) | collective-permute-done | bytes 163872 | tf_op jit(solution)/shard_map/ppermute | solution.py:555
  52.6 1.1 %shard_map.88 = (f32[3,3,3,32,40]{4,3,2,1,0:T(8,128)}, bf16[4,64,320]{2,1,0:T(8,128)(2,1)}) custom-call(f32[8,128]{1,0:T(8,128)S(1)} %get-tuple-element.48.refs_0_, f32[192,128]{1,0:T(8,128)S(1)} %shard_map.85.refs_0_.refs_1_, f32[192,128]{1,0:T(8,128)S(1)} %collective-permute-done.14.refs_2_, bf16[4,64,320]{2,1,0:T(8,128)(2,1)S(1)} %get-tuple-element.38.refs_0_.refs_3_, ...), custom_call_target="tpu_custom_call" | custom-call | flops 1150000000 | bytes 3700000 | tf_op jit(solution)/shard_map/pallas_call | solution.py:539
  (3 shorter events, 0.1 us)
Async XLA Ops:
  0.6 9.6 %collective-permute-start.2 = (bf16[4,64,320]{2,1,0:T(8,128)(2,1)}, bf16[4,64,320]{2,1,0:T(8,128)(2,1)S(1)}, u32[]{:S(2)}, u32[]{:S(2)}) collective-permute-start(bf16[4,64,320]{2,1,0:T(8,128)(2,1)} %refs_1_.5), channel_id=1, source_target_pairs={{0,2},{1,3},{2,4},{3,5},{4,6},{5,7},{6,8},{7,9},{8,10},{9,11},{10,... | collective-permute-start | bytes 491528 | tf_op jit(solution)/shard_map/ppermute | solution.py:555
  5.5 0.9 %copy-start = (bf16[4,64,320]{2,1,0:T(8,128)(2,1)S(1)}, bf16[4,64,320]{2,1,0:T(8,128)(2,1)}, u32[]{:S(2)}) copy-start(bf16[4,64,320]{2,1,0:T(8,128)(2,1)} %refs_1_.5) | copy-start | bytes 491524
  6.5 1.1 %copy-start.2 = (bf16[24,4,64,32]{2,3,1,0:T(8,128)(2,1)S(1)}, bf16[24,4,64,32]{2,3,1,0:T(8,128)(2,1)}, u32[]{:S(2)}) copy-start(bf16[24,4,64,32]{2,3,1,0:T(8,128)(2,1)} %param.7) | copy-start | bytes 1179652
  7.6 0.9 %copy-start.4 = (bf16[4,64,320]{2,1,0:T(8,128)(2,1)S(1)}, bf16[4,64,320]{2,1,0:T(8,128)(2,1)}, u32[]{:S(2)}) copy-start(bf16[4,64,320]{2,1,0:T(8,128)(2,1)} %refs_0_.3) | copy-start | bytes 491524
  8.5 1.7 %copy-start.1 = (bf16[4,64,320]{2,1,0:T(8,128)(2,1)S(1)}, bf16[4,64,320]{2,1,0:T(8,128)(2,1)}, u32[]{:S(2)}) copy-start(bf16[4,64,320]{2,1,0:T(8,128)(2,1)} %refs_1_.5) | copy-start | bytes 491524
  8.5 7.8 %copy-start.5 = (bf16[4,64,320]{2,1,0:T(8,128)(2,1)S(1)}, bf16[4,64,320]{2,1,0:T(8,128)(2,1)}, u32[]{:S(2)}) copy-start(bf16[4,64,320]{2,1,0:T(8,128)(2,1)} %refs_0_.3) | copy-start | bytes 491524
  8.9 1.3 %collective-permute-start = (bf16[32,320]{1,0:T(8,128)(2,1)S(1)}, bf16[32,320]{1,0:T(8,128)(2,1)S(1)}, u32[]{:S(2)}, u32[]{:S(2)}) collective-permute-start(bf16[32,320]{1,0:T(8,128)(2,1)S(1)} %get-tuple-element.28), channel_id=1, source_target_pairs={{0,1},{1,0},{2,3},{3,2},{4,5},{5,4},{6,7},{7,6},{8,9},{9,8},{10,11... | collective-permute-start | bytes 61448 | tf_op jit(solution)/shard_map/ppermute | solution.py:611
  8.9 1.2 %collective-permute-start.1 = (bf16[32,320]{1,0:T(8,128)(2,1)S(1)}, bf16[32,320]{1,0:T(8,128)(2,1)S(1)}, u32[]{:S(2)}, u32[]{:S(2)}) collective-permute-start(bf16[32,320]{1,0:T(8,128)(2,1)S(1)} %get-tuple-element.29), channel_id=1, source_target_pairs={{1,2},{3,4},{5,6},{7,8},{9,10},{11,12},{13,14},{2,1},{4,3},{6,5},{... | collective-permute-start | bytes 61448 | tf_op jit(solution)/shard_map/ppermute | solution.py:630
  10.3 6.0 %collective-permute-start.3 = (bf16[4,64,320]{2,1,0:T(8,128)(2,1)S(1)}, bf16[4,64,320]{2,1,0:T(8,128)(2,1)S(1)}, u32[]{:S(2)}, u32[]{:S(2)}) collective-permute-start(bf16[4,64,320]{2,1,0:T(8,128)(2,1)S(1)} %shard_map.77), channel_id=1, source_target_pairs={{0,1},{1,0},{2,3},{3,2},{4,5},{5,4},{6,7},{7,6},{8,9},{9,8},{10,11... | collective-permute-start | bytes 491528 | tf_op jit(solution)/shard_map/ppermute | solution.py:611
  14.8 5.3 %collective-permute-start.4 = (bf16[6,80,128]{2,1,0:T(8,128)(2,1)S(1)}, bf16[6,80,128]{2,1,0:T(8,128)(2,1)S(1)}, u32[]{:S(2)}, u32[]{:S(2)}) collective-permute-start(bf16[6,80,128]{2,1,0:T(8,128)(2,1)S(1)} %shard_map.76.refs_0_), channel_id=1, source_target_pairs={{0,16},{16,0},{1,17},{17,1},{2,18},{18,2},{3,19},{19,3},{4,20},{20... | collective-permute-start | bytes 368648 | tf_op jit(solution)/shard_map/ppermute | solution.py:566
  20.1 3.7 %copy-start.3 = (bf16[3,3,3,40,32]{3,4,2,1,0:T(8,128)(2,1)S(1)}, bf16[3,3,3,40,32]{3,4,2,1,0:T(8,128)(2,1)}, u32[]{:S(2)}) copy-start(bf16[3,3,3,40,32]{3,4,2,1,0:T(8,128)(2,1)} %param.6) | copy-start | bytes 207364
  22.2 2.5 %collective-permute-start.5 = (f32[192,128]{1,0:T(8,128)S(1)}, f32[192,128]{1,0:T(8,128)S(1)}, u32[]{:S(2)}, u32[]{:S(2)}) collective-permute-start(f32[192,128]{1,0:T(8,128)S(1)} %get-tuple-element.35), channel_id=1, source_target_pairs={{0,1},{1,0},{2,3},{3,2},{4,5},{5,4},{6,7},{7,6},{8,9},{9,8},{10,11... | collective-permute-start | bytes 294920 | tf_op jit(solution)/shard_map/ppermute | solution.py:611
  22.2 22.5 %collective-permute-start.13 = (bf16[960,128]{1,0:T(8,128)(2,1)S(1)}, bf16[960,128]{1,0:T(8,128)(2,1)S(1)}, u32[]{:S(2)}, u32[]{:S(2)}) collective-permute-start(bf16[960,128]{1,0:T(8,128)(2,1)S(1)} %get-tuple-element.45), channel_id=1, source_target_pairs={{0,16},{16,0},{1,17},{17,1},{2,18},{18,2},{3,19},{19,3},{4,20},{20... | collective-permute-start | bytes 737288 | tf_op jit(solution)/shard_map/ppermute | solution.py:566
  24.7 7.1 %collective-permute-start.6 = (bf16[192,128]{1,0:T(8,128)(2,1)S(1)}, bf16[192,128]{1,0:T(8,128)(2,1)S(1)}, u32[]{:S(2)}, u32[]{:S(2)}) collective-permute-start(bf16[192,128]{1,0:T(8,128)(2,1)S(1)} %shard_map.81.refs_0_.refs_1_), channel_id=1, source_target_pairs={{0,2},{1,3},{2,0},{3,1},{4,6},{5,7},{6,4},{7,5},{8,10},{9,11},{10,... | collective-permute-start | bytes 147464 | tf_op jit(solution)/shard_map/ppermute | solution.py:611
  27.1 5.0 %collective-permute-start.7 = (bf16[192,128]{1,0:T(8,128)(2,1)S(1)}, bf16[192,128]{1,0:T(8,128)(2,1)S(1)}, u32[]{:S(2)}, u32[]{:S(2)}) collective-permute-start(bf16[192,128]{1,0:T(8,128)(2,1)S(1)} %shard_map.81.refs_0_.refs_1_), channel_id=1, source_target_pairs={{0,16},{1,17},{2,18},{3,19},{4,20},{5,21},{6,22},{7,23},{8,24},{9,... | collective-permute-start | bytes 147464 | tf_op jit(solution)/shard_map/ppermute | solution.py:611
  27.7 6.9 %collective-permute-start.8 = (bf16[192,128]{1,0:T(8,128)(2,1)S(1)}, bf16[192,128]{1,0:T(8,128)(2,1)S(1)}, u32[]{:S(2)}, u32[]{:S(2)}) collective-permute-start(bf16[192,128]{1,0:T(8,128)(2,1)S(1)} %shard_map.81.refs_0_.refs_1_), channel_id=1, source_target_pairs={{0,18},{1,19},{2,16},{3,17},{4,22},{5,23},{6,20},{7,21},{8,26},{9,... | collective-permute-start | bytes 147464 | tf_op jit(solution)/shard_map/ppermute | solution.py:611
  31.7 11.6 %collective-permute-start.12 = (bf16[4,64,320]{2,1,0:T(8,128)(2,1)S(1)}, bf16[4,64,320]{2,1,0:T(8,128)(2,1)S(1)}, u32[]{:S(2)}, u32[]{:S(2)}) collective-permute-start(bf16[4,64,320]{2,1,0:T(8,128)(2,1)S(1)} %get-tuple-element.43), channel_id=1, source_target_pairs={{0,1},{1,0},{2,3},{3,2},{4,5},{5,4},{6,7},{7,6},{8,9},{9,8},{10,11... | collective-permute-start | bytes 491528 | tf_op jit(solution)/shard_map/ppermute | solution.py:611
  34.6 6.3 %collective-permute-start.10 = (bf16[192,128]{1,0:T(8,128)(2,1)S(1)}, bf16[192,128]{1,0:T(8,128)(2,1)S(1)}, u32[]{:S(2)}, u32[]{:S(2)}) collective-permute-start(bf16[192,128]{1,0:T(8,128)(2,1)S(1)} %shard_map.83.refs_0_.refs_1_), channel_id=1, source_target_pairs={{0,8},{1,9},{2,10},{3,11},{4,12},{5,13},{6,14},{7,15},{8,0},{9,1},... | collective-permute-start | bytes 147464 | tf_op jit(solution)/shard_map/ppermute | solution.py:611
  37.3 6.0 %collective-permute-start.11 = (bf16[192,128]{1,0:T(8,128)(2,1)S(1)}, bf16[192,128]{1,0:T(8,128)(2,1)S(1)}, u32[]{:S(2)}, u32[]{:S(2)}) collective-permute-start(bf16[192,128]{1,0:T(8,128)(2,1)S(1)} %shard_map.83.refs_0_.refs_1_), channel_id=1, source_target_pairs={{0,12},{1,13},{2,14},{3,15},{4,8},{5,9},{6,10},{7,11},{8,4},{9,5},... | collective-permute-start | bytes 147464 | tf_op jit(solution)/shard_map/ppermute | solution.py:611
  38.6 4.6 %collective-permute-start.9 = (bf16[192,128]{1,0:T(8,128)(2,1)S(1)}, bf16[192,128]{1,0:T(8,128)(2,1)S(1)}, u32[]{:S(2)}, u32[]{:S(2)}) collective-permute-start(bf16[192,128]{1,0:T(8,128)(2,1)S(1)} %shard_map.83.refs_0_.refs_1_), channel_id=1, source_target_pairs={{0,4},{1,5},{2,6},{3,7},{4,0},{5,1},{6,2},{7,3},{8,12},{9,13},{10,... | collective-permute-start | bytes 147464 | tf_op jit(solution)/shard_map/ppermute | solution.py:611
  43.2 5.4 %collective-permute-start.14 = (f32[192,128]{1,0:T(8,128)S(1)}, f32[192,128]{1,0:T(8,128)S(1)}, u32[]{:S(2)}, u32[]{:S(2)}) collective-permute-start(f32[192,128]{1,0:T(8,128)S(1)} %shard_map.85.refs_0_.refs_1_), channel_id=1, source_target_pairs={{0,1},{1,0},{2,3},{3,2},{4,5},{5,4},{6,7},{7,6},{8,9},{9,8},{10,11... | collective-permute-start | bytes 294920 | tf_op jit(solution)/shard_map/ppermute | solution.py:611
  43.4 9.2 %collective-permute-start.15 = (bf16[4,64,320]{2,1,0:T(8,128)(2,1)S(1)}, bf16[4,64,320]{2,1,0:T(8,128)(2,1)S(1)}, u32[]{:S(2)}, u32[]{:S(2)}) collective-permute-start(bf16[4,64,320]{2,1,0:T(8,128)(2,1)S(1)} %shard_map.86.refs_1_), channel_id=1, source_target_pairs={{2,0},{3,1},{4,2},{5,3},{6,4},{7,5},{8,6},{9,7},{10,8},{11,9},{12,... | collective-permute-start | bytes 491528 | tf_op jit(solution)/shard_map/ppermute | solution.py:555

commit v2 on v1

--- a/solution.py
+++ b/solution.py
@@ -454,6 +454,12 @@
     right[...] = (own[...].astype(F32) + beside + far[...].astype(F32)).astype(BF16)
 
 
+def copy_kernel(*refs):
+    half = len(refs) // 2
+    for src, dst in zip(refs[:half], refs[half:]):
+        dst[...] = src[...]
+
+
 def sum_kernel(*refs):
     *parts, out = refs
     out[...] = tree([ref[...].astype(F32) for ref in parts]).astype(out.dtype)
@@ -628,6 +634,17 @@
     inner = range(1, n_col - 1, 2)
     by_even = swap(by_even, 1)
     by_odd = lax.ppermute(by_odd, "col", [(i, i + 1) for i in inner] + [(i + 1, i) for i in inner])
+    (passed,) = call(
+        pass_kernel, [((rows, cols, channels), BF16)], [], right_features, far, after=[ctl]
+    )
+    near = swap(passed, 1)
+    w2, wc = call(
+        taps_kernel,
+        [((12 * 128, 2 * 128), BF16), ((4 * 3 * rows * SLOT, 2 * rows * feat), BF16)],
+        [pltpu.VMEM((3 * rows * feat, 3 * rows * SLOT), F32)],
+        conv_weight.transpose(0, 1, 2, 4, 3),
+        after=[passed],
+    )
     row_pays = call(
         functools.partial(row_kernel, ends, rows),
         [((disp // per, total, 128), BF16)] * n,
@@ -635,12 +652,10 @@
         by_even,
         by_odd,
         *rims,
+        after=[w2],
+        us=5.0,
     )
     top, bot = halos(row_pays)
-    (near,) = call(
-        pass_kernel, [((rows, cols, channels), BF16)], [], right_features, far, after=row_pays
-    )
-    near = swap(near, 1)
 
     band = 104 + cols + PAD
     spread_rows = 3 * rows * cols + rows * cols // 2 + 2 * count
@@ -665,8 +680,6 @@
         by_odd,
         us=2.3,
     )
-    vtop, vbot = halos(volume_rows)
-
     keep, give, ctsh = call(
         functools.partial(weight_kernel, masks, groups, feat),
         [((3 * 64, 128), F32), ((3 * 64, 128), F32), ((disp // 2 + 1, 2, cols, 3 * 256), BF16)],
@@ -679,15 +692,7 @@
         us=2.6,
     )
     got = swap(give, 1)
-    w2, wc = call(
-        taps_kernel,
-        [((12 * 128, 2 * 128), BF16), ((4 * 3 * rows * SLOT, 2 * rows * feat), BF16)],
-        [pltpu.VMEM((3 * rows * feat, 3 * rows * SLOT), F32)],
-        conv_weight.transpose(0, 1, 2, 4, 3),
-        after=[keep],
-        us=0.8,
-    )
-    (part,) = call(sum_kernel, [(keep.shape, BF16)], [], keep, got, after=[w2])
+    (part,) = call(sum_kernel, [(keep.shape, BF16)], [], keep, got)
     gv, rg0, rg1, rg2 = call(
         right_kernel,
         [
@@ -710,20 +715,24 @@
     order = [rg0]
     for stage in middle:
         parts = [part] + [swap(part, m) for m in stage]
-        (part,) = call(sum_kernel, [(part.shape, BF16)], [], *parts, after=order)
+        (part,) = call(sum_kernel, [(part.shape, BF16)], [], *parts, after=order, us=4.0)
         order = []
+    volume_rows = call(
+        copy_kernel, [(x.shape, x.dtype) for x in volume_rows], [], *volume_rows, after=[part]
+    )
+    vtop, vbot = halos(volume_rows)
     parts = [part] + [swap(part, m) for m in final]
+    (rg2,) = call(
+        combine_kernel, [((rows, cols, channels), BF16)], [], rg1, rg2, after=volume_rows
+    )
     lg, left_done = call(
         left_kernel,
         [((rows, cols, channels), BF16)],
         [pltpu.VMEM((rows, cols, wide), F32)],
         gv, fr, fr4,
-        after=[part],
+        after=[rg2],
         token=True,
         us=1.9,
-    )
-    (rg2,) = call(
-        combine_kernel, [((rows, cols, channels), BF16)], [], rg1, rg2, after=[left_done]
     )
     (part,) = call(sum_kernel, [(part.shape, F32)], [], *parts, after=[left_done])
     output, conv_done = call(
@@ -734,7 +743,7 @@
             pltpu.VMEM((rows // 2, disp, total, 128), F32),
         ],
         vbuf, vtop, vbot, wc,
-        after=[part, rg2],
+        after=[part],
         token=True,
         us=3.9,
     )

time: 53.9 us -> 46.3 us (0.86)
  waiting for transfers between devices: 11.3 us -> 5.25 us
  starting transfers between devices: 22.7 us -> 21 us
    ppermute x2, waiting for transfers between devices: 3.94 us -> 0.37 us  [col_shift(): return lax.ppermute(block, 'col', route)]
    ppermute x11, waiting for transfers between devices: 5.98 us -> 2.59 us  [swap(): return lax.ppermute(block, ('row', 'col'), route)]
    ppermute x11, starting transfers between devices: 12.8 us -> 10.9 us  [swap(): return lax.ppermute(block, ('row', 'col'), route)]
    ppermute x2, waiting for transfers between devices: 1.41 us -> 2.28 us  [halos(): got = lax.ppermute(pays[0], 'row', [(0, 1), (1, 0)])]
    pallas_call x14 -> x15, Pallas kernels: 15.8 us -> 15.8 us  [call(): pl.pallas_call(lambda *refs: kernel(*refs[skip:]), out_shape=[jax.ShapeDt...]
  transfers between devices with their start and end apart: 16 -> 16, of which waited for: 7 -> 6; matrix products, arithmetic and copies ran while one was open for 0% -> 0% of each run, Pallas kernels for 24% -> 28%
where the time goes in v2:
time: 46.3 us; the launch traced here: 45.8 us
  starting transfers between devices  21 us (45%)
  Pallas kernels  15.8 us (34%)
  waiting for transfers between devices  5.25 us (11%)
  local copies, waits for them, and re-layouts  3 us (6%)
  between operations  0.82 us (2%)
    pallas_call x15, Pallas kernels, call(): pl.pallas_call(lambda *refs: kernel(*refs[skip:]), out_shape=[jax.ShapeDt...  15.8 us
    ppermute x11, starting transfers between devices, swap(): return lax.ppermute(block, ('row', 'col'), route)  10.9 us
    ppermute x2, starting transfers between devices, col_shift(): return lax.ppermute(block, 'col', route)  6.31 us
    ppermute x2, starting transfers between devices, halos(): got = lax.ppermute(pays[0], 'row', [(0, 1), (1, 0)])  3.11 us
    unnamed x12, local copies, waits for them, and re-layouts  3 us
    ppermute x11, waiting for transfers between devices, swap(): return lax.ppermute(block, ('row', 'col'), route)  2.59 us
    ppermute x2, waiting for transfers between devices, halos(): got = lax.ppermute(pays[0], 'row', [(0, 1), (1, 0)])  2.28 us
  transfers between devices with their start and end apart: 16, of which 6 were waited for; matrix products, arithmetic and copies ran while one was open for 0% of the time, Pallas kernels for 28%

profile of v2, /device:TPU:0, one launch (start us, length us, event | category | flops | bytes accessed | tf_op | source)
XLA Modules:
  0.0 45.8 jit_solution(5072915556102140444)
XLA Ops:
  0.6 0.0 copy-start
  0.6 5.0 %collective-permute-start = (bf16[4,64,320]{2,1,0:T(8,128)(2,1)}, bf16[4,64,320]{2,1,0:T(8,128)(2,1)S(1)}, u32[]{:S(2)}, u32[]{:S(2)}) collective-permute-start(bf16[4,64,320]{2,1,0:T(8,128)(2,1)} %refs_1_.5), channel_id=1, source_target_pairs={{0,2},{1,3},{2,4},{3,5},{4,6},{5,7},{6,8},{7,9},{8,10},{9,11},{10,... | collective-permute-start | bytes 491528 | tf_op jit(solution)/shard_map/ppermute | solution.py:561
  5.7 0.0 copy-start.1
  5.7 0.9 %copy-done.1 = bf16[4,64,320]{2,1,0:T(8,128)(2,1)S(1)} copy-done((bf16[4,64,320]{2,1,0:T(8,128)(2,1)S(1)}, bf16[4,64,320]{2,1,0:T(8,128)(2,1)}, u32[]{:S(2)}) %copy-start.1) | copy-done | bytes 163864
  6.6 0.0 copy-start.3
  6.6 1.1 %copy-done.3 = bf16[24,4,64,32]{2,3,1,0:T(8,128)(2,1)S(1)} copy-done((bf16[24,4,64,32]{2,3,1,0:T(8,128)(2,1)S(1)}, bf16[24,4,64,32]{2,3,1,0:T(8,128)(2,1)}, u32[]{:S(2)}) %copy-start.3) | copy-done | bytes 393240
  7.7 0.0 copy-start.4
  7.7 0.9 %copy-done.4 = bf16[4,64,320]{2,1,0:T(8,128)(2,1)S(1)} copy-done((bf16[4,64,320]{2,1,0:T(8,128)(2,1)S(1)}, bf16[4,64,320]{2,1,0:T(8,128)(2,1)}, u32[]{:S(2)}) %copy-start.4) | copy-done | bytes 163864
  8.7 0.3 shard_map.75
  9.0 0.1 collective-permute-start.2
  9.1 0.7 %collective-permute-start.3 = (bf16[32,320]{1,0:T(8,128)(2,1)S(1)}, bf16[32,320]{1,0:T(8,128)(2,1)S(1)}, u32[]{:S(2)}, u32[]{:S(2)}) collective-permute-start(bf16[32,320]{1,0:T(8,128)(2,1)S(1)} %get-tuple-element.30), channel_id=1, source_target_pairs={{1,2},{3,4},{5,6},{7,8},{9,10},{11,12},{13,14},{2,1},{4,3},{6,5},{... | collective-permute-start | bytes 61448 | tf_op jit(solution)/shard_map/ppermute | solution.py:636
  9.7 0.4 collective-permute-done.refs_2_.refs_3_
  10.1 0.1 shard_map.76.refs_0_
  10.2 2.6 %collective-permute-start.1 = (bf16[4,64,320]{2,1,0:T(8,128)(2,1)S(1)}, bf16[4,64,320]{2,1,0:T(8,128)(2,1)S(1)}, u32[]{:S(2)}, u32[]{:S(2)}) collective-permute-start(bf16[4,64,320]{2,1,0:T(8,128)(2,1)S(1)} %shard_map.76.refs_0_), channel_id=1, source_target_pairs={{0,1},{1,0},{2,3},{3,2},{4,5},{5,4},{6,7},{7,6},{8,9},{9,8},{10,11... | collective-permute-start | bytes 491528 | tf_op jit(solution)/shard_map/ppermute | solution.py:617
  12.8 0.0 copy-done
  12.8 0.8 %shard_map.78 = (bf16[1536,256]{1,0:T(8,128)(2,1)S(1)}, bf16[3072,256]{1,0:T(8,128)(2,1)S(1)}) custom-call(bf16[4,64,320]{2,1,0:T(8,128)(2,1)S(1)} %shard_map.76.refs_0_, bf16[3,3,3,32,40]{4,3,2,1,0:T(8,128)(2,1)S(1)} %bitcast.4), custom_call_target="tpu_custom_call" | custom-call | tf_op jit(solution)/shard_map/pallas_call | solution.py:545
  13.6 0.0 collective-permute-done.2.refs_4_.refs_1_.refs_2_
  13.6 0.0 collective-permute-done.3.refs_5_.refs_2_.refs_3_
  13.6 0.0 copy-start.2
  13.6 0.0 copy-start.5
  13.7 0.1 shard_map.79
  13.8 1.6 %collective-permute-start.4 = (bf16[6,80,128]{2,1,0:T(8,128)(2,1)S(1)}, bf16[6,80,128]{2,1,0:T(8,128)(2,1)S(1)}, u32[]{:S(2)}, u32[]{:S(2)}) collective-permute-start(bf16[6,80,128]{2,1,0:T(8,128)(2,1)S(1)} %shard_map.79), channel_id=1, source_target_pairs={{0,16},{16,0},{1,17},{17,1},{2,18},{18,2},{3,19},{19,3},{4,20},{20... | collective-permute-start | bytes 368648 | tf_op jit(solution)/shard_map/ppermute | solution.py:572
  15.3 0.0 collective-permute-done.1.refs_2_
  15.3 0.0 copy-done.2
  15.3 0.0 copy-done.5
  15.3 2.3 %shard_map.77 = (f32[2,24,80,128]{3,2,1,0:T(8,128)S(1)}, f32[4,80,512]{2,1,0:T(8,128)S(1)}, f32[4,176,512]{2,1,0:T(8,128)S(1)}, f32[4,176,512]{2,1,0:T(8,128)S(1)}, bf16[960,128]{1,0:T(8,128)(2,1)S(1)}) custom-call(bf16[4,64,320]{2,1,0:T(8,128)(2,1)S(1)} %copy-done.5, bf16[4,64,320]{2,1,0:T(8,128)(2,1)S(1)} %copy-done.2, ...), custom_call_target="tpu_custom_call" | custom-call | flops 2644999936 | bytes 8510000 | tf_op jit(solution)/shard_map/pallas_call | solution.py:545
  17.7 2.3 %collective-permute-done.4.refs_4_.refs_5_ = bf16[6,80,128]{2,1,0:T(8,128)(2,1)S(1)} collective-permute-done((bf16[6,80,128]{2,1,0:T(8,128)(2,1)S(1)}, bf16[6,80,128]{2,1,0:T(8,128)(2,1)S(1)}, u32[]{:S(2)}, u32[]{:S(2)}) %collective-permute-start.4) | collective-permute-done | bytes 122912 | tf_op jit(solution)/shard_map/ppermute | solution.py:572
  20.0 2.0 %shard_map.80 = (f32[192,128]{1,0:T(8,128)S(1)}, f32[192,128]{1,0:T(8,128)S(1)}, bf16[13,2,64,768]{3,2,1,0:T(8,128)(2,1)S(1)}) custom-call(f32[2,24,80,128]{3,2,1,0:T(8,128)S(1)} %get-tuple-element.31.refs_0_.refs_1_, bf16[24,64,128]{2,1,0:T(8,128)(2,1)S(1)} %get-tuple-element.28.refs_0_.refs_1_, ...), custom_call_target="tpu_custom_call" | custom-call | flops 2990000128 | bytes 9620000 | tf_op jit(solution)/shard_map/pallas_call | solution.py:545
  22.0 0.2 collective-permute-start.5
  22.2 1.2 %collective-permute-done.5.refs_1_ = f32[192,128]{1,0:T(8,128)S(1)} collective-permute-done((f32[192,128]{1,0:T(8,128)S(1)}, f32[192,128]{1,0:T(8,128)S(1)}, u32[]{:S(2)}, u32[]{:S(2)}) %collective-permute-start.5) | collective-permute-done | bytes 98336 | tf_op jit(solution)/shard_map/ppermute | solution.py:617
  23.4 2.8 %collective-permute-start.8 = (bf16[192,128]{1,0:T(8,128)(2,1)S(1)}, bf16[192,128]{1,0:T(8,128)(2,1)S(1)}, u32[]{:S(2)}, u32[]{:S(2)}) collective-permute-start(bf16[192,128]{1,0:T(8,128)(2,1)S(1)} %shard_map.81.refs_0_.refs_1_), channel_id=1, source_target_pairs={{0,18},{1,19},{2,16},{3,17},{4,22},{5,23},{6,20},{7,21},{8,26},{9,... | collective-permute-start | bytes 147464 | tf_op jit(solution)/shard_map/ppermute | solution.py:617
  26.2 0.5 %collective-permute-start.7 = (bf16[192,128]{1,0:T(8,128)(2,1)S(1)}, bf16[192,128]{1,0:T(8,128)(2,1)S(1)}, u32[]{:S(2)}, u32[]{:S(2)}) collective-permute-start(bf16[192,128]{1,0:T(8,128)(2,1)S(1)} %shard_map.81.refs_0_.refs_1_), channel_id=1, source_target_pairs={{0,16},{1,17},{2,18},{3,19},{4,20},{5,21},{6,22},{7,23},{8,24},{9,... | collective-permute-start | bytes 147464 | tf_op jit(solution)/shard_map/ppermute | solution.py:617
  26.7 0.2 collective-permute-start.6
  26.9 3.0 %shard_map.82 = (f32[4,24,64,128]{3,2,1,0:T(8,128)S(1)}, bf16[4,64,320]{2,1,0:T(8,128)(2,1)S(1)}, bf16[4,64,320]{2,1,0:T(8,128)(2,1)S(1)}, bf16[4,32,320]{2,1,0:T(8,128)(2,1)S(1)}) custom-call(bf16[192,128]{1,0:T(8,128)(2,1)S(1)} %shard_map.81.refs_0_.refs_1_, bf16[13,2,64,768]{3,2,1,0:T(8,128)(2,1)S(1)} %get-tuple-element.36.refs_1_, ...), custom_call_target="tpu_custom_call" | custom-call | flops 3335000064 | bytes 10730000 | tf_op jit(solution)/shard_map/pallas_call | solution.py:545
  29.9 0.1 collective-permute-start.9
  30.0 0.0 collective-permute-done.8.refs_4_
  30.0 0.2 collective-permute-done.7.refs_3_
  30.3 0.5 %collective-permute-done.6.refs_2_ = bf16[192,128]{1,0:T(8,128)(2,1)S(1)} collective-permute-done((bf16[192,128]{1,0:T(8,128)(2,1)S(1)}, bf16[192,128]{1,0:T(8,128)(2,1)S(1)}, u32[]{:S(2)}, u32[]{:S(2)}) %collective-permute-start.6) | collective-permute-done | bytes 49184 | tf_op jit(solution)/shard_map/ppermute | solution.py:617
  30.9 1.6 %collective-permute-start.13 = (bf16[960,128]{1,0:T(8,128)(2,1)S(1)}, bf16[960,128]{1,0:T(8,128)(2,1)S(1)}, u32[]{:S(2)}, u32[]{:S(2)}) collective-permute-start(bf16[960,128]{1,0:T(8,128)(2,1)S(1)} %shard_map.84.refs_0_), channel_id=1, source_target_pairs={{0,16},{16,0},{1,17},{17,1},{2,18},{18,2},{3,19},{19,3},{4,20},{20... | collective-permute-start | bytes 737288 | tf_op jit(solution)/shard_map/ppermute | solution.py:572
  32.4 3.3 %collective-permute-start.12 = (bf16[192,128]{1,0:T(8,128)(2,1)S(1)}, bf16[192,128]{1,0:T(8,128)(2,1)S(1)}, u32[]{:S(2)}, u32[]{:S(2)}) collective-permute-start(bf16[192,128]{1,0:T(8,128)(2,1)S(1)} %shard_map.83.refs_0_.refs_1_), channel_id=1, source_target_pairs={{0,12},{1,13},{2,14},{3,15},{4,8},{5,9},{6,10},{7,11},{8,4},{9,5},... | collective-permute-start | bytes 147464 | tf_op jit(solution)/shard_map/ppermute | solution.py:617
  35.7 0.0 collective-permute-start.11
  35.7 1.1 %collective-permute-start.10 = (bf16[192,128]{1,0:T(8,128)(2,1)S(1)}, bf16[192,128]{1,0:T(8,128)(2,1)S(1)}, u32[]{:S(2)}, u32[]{:S(2)}) collective-permute-start(bf16[192,128]{1,0:T(8,128)(2,1)S(1)} %shard_map.83.refs_0_.refs_1_), channel_id=1, source_target_pairs={{0,4},{1,5},{2,6},{3,7},{4,0},{5,1},{6,2},{7,3},{8,12},{9,13},{10,... | collective-permute-start | bytes 147464 | tf_op jit(solution)/shard_map/ppermute | solution.py:617
  36.8 0.0 collective-permute-done.9.refs_1_.refs_4_
  36.8 0.1 shard_map.85.refs_0_
  36.9 1.3 %collective-permute-start.15 = (bf16[4,64,320]{2,1,0:T(8,128)(2,1)S(1)}, bf16[4,64,320]{2,1,0:T(8,128)(2,1)S(1)}, u32[]{:S(2)}, u32[]{:S(2)}) collective-permute-start(bf16[4,64,320]{2,1,0:T(8,128)(2,1)S(1)} %shard_map.85.refs_0_), channel_id=1, source_target_pairs={{2,0},{3,1},{4,2},{5,3},{6,4},{7,5},{8,6},{9,7},{10,8},{11,9},{12,... | collective-permute-start | bytes 491528 | tf_op jit(solution)/shard_map/ppermute | solution.py:561
  38.2 1.9 %shard_map.86 = (bf16[4,64,320]{2,1,0:T(8,128)(2,1)}, f32[8,128]{1,0:T(8,128)S(1)}) custom-call(bf16[4,64,320]{2,1,0:T(8,128)(2,1)S(1)} %shard_map.85.refs_0_, f32[4,24,64,128]{3,2,1,0:T(8,128)S(1)} %get-tuple-element.42.refs_1_, f32[4,176,512]{2,1,0:T(8,128)S(1)} %get-tuple-element.43.refs_2_, f32[4,176,512]{2,1,0:T(8,128)S(1)} %get-tuple-element.44.refs_3_), custom_call_target="tpu_custom_call" | custom-call | flops 2184999936 | bytes 7030000 | tf_op jit(solution)/shard_map/pallas_call | solution.py:545
  40.1 0.0 collective-permute-done.12.refs_4_
  40.1 0.6 %collective-permute-done.11.refs_3_ = bf16[192,128]{1,0:T(8,128)(2,1)S(1)} collective-permute-done((bf16[192,128]{1,0:T(8,128)(2,1)S(1)}, bf16[192,128]{1,0:T(8,128)(2,1)S(1)}, u32[]{:S(2)}, u32[]{:S(2)}) %collective-permute-start.11) | collective-permute-done | bytes 49184 | tf_op jit(solution)/shard_map/ppermute | solution.py:617
  40.7 0.0 collective-permute-done.10.refs_2_
  40.7 0.1 collective-permute-start.14
  40.8 0.0 collective-permute-done.13.refs_2_.refs_3_
  40.8 3.9 %shard_map.88 = (bf16[24,4,32,64]{3,2,1,0:T(8,128)(2,1)}, f32[8,128]{1,0:T(8,128)S(1)}) custom-call(f32[192,128]{1,0:T(8,128)S(1)} %shard_map.87.refs_0_.refs_1_, f32[2,24,80,128]{3,2,1,0:T(8,128)S(1)} %get-tuple-element.31.refs_0_.refs_1_, bf16[960,128]{1,0:T(8,128)(2,1)S(1)} %collective-permute-done.13.refs_2_.refs_3_, ...), custom_call_target="tpu_custom_call" | custom-call | flops 4485000192 | bytes 14430000 | tf_op jit(solution)/shard_map/pallas_call | solution.py:545
  44.8 0.0 collective-permute-done.14.refs_2_
  44.8 0.0 collective-permute-done.15.refs_5_
  44.8 1.1 %shard_map.89 = (f32[3,3,3,32,40]{4,3,2,1,0:T(8,128)}, bf16[4,64,320]{2,1,0:T(8,128)(2,1)}) custom-call(f32[8,128]{1,0:T(8,128)S(1)} %get-tuple-element.48.refs_0_, f32[192,128]{1,0:T(8,128)S(1)} %shard_map.87.refs_0_.refs_1_, f32[192,128]{1,0:T(8,128)S(1)} %collective-permute-done.14.refs_2_, bf16[4,64,320]{2,1,0:T(8,128)(2,1)S(1)} %get-tuple-element.38.refs_0_.refs_3_, ...), custom_call_target="tpu_custom_call" | custom-call | flops 1150000000 | bytes 3700000 | tf_op jit(solution)/shard_map/pallas_call | solution.py:545
  (4 shorter events, 0.1 us)
Async XLA Ops:
  0.6 12.1 %copy-start = (bf16[3,3,3,40,32]{3,4,2,1,0:T(8,128)(2,1)S(1)}, bf16[3,3,3,40,32]{3,4,2,1,0:T(8,128)(2,1)}, u32[]{:S(2)}) copy-start(bf16[3,3,3,40,32]{3,4,2,1,0:T(8,128)(2,1)} %param.6) | copy-start | bytes 207364
  0.6 9.5 %collective-permute-start = (bf16[4,64,320]{2,1,0:T(8,128)(2,1)}, bf16[4,64,320]{2,1,0:T(8,128)(2,1)S(1)}, u32[]{:S(2)}, u32[]{:S(2)}) collective-permute-start(bf16[4,64,320]{2,1,0:T(8,128)(2,1)} %refs_1_.5), channel_id=1, source_target_pairs={{0,2},{1,3},{2,4},{3,5},{4,6},{5,7},{6,8},{7,9},{8,10},{9,11},{10,... | collective-permute-start | bytes 491528 | tf_op jit(solution)/shard_map/ppermute | solution.py:561
  5.7 0.9 %copy-start.1 = (bf16[4,64,320]{2,1,0:T(8,128)(2,1)S(1)}, bf16[4,64,320]{2,1,0:T(8,128)(2,1)}, u32[]{:S(2)}) copy-start(bf16[4,64,320]{2,1,0:T(8,128)(2,1)} %refs_1_.5) | copy-start | bytes 491524
  6.6 1.1 %copy-start.3 = (bf16[24,4,64,32]{2,3,1,0:T(8,128)(2,1)S(1)}, bf16[24,4,64,32]{2,3,1,0:T(8,128)(2,1)}, u32[]{:S(2)}) copy-start(bf16[24,4,64,32]{2,3,1,0:T(8,128)(2,1)} %param.7) | copy-start | bytes 1179652
  7.7 0.9 %copy-start.4 = (bf16[4,64,320]{2,1,0:T(8,128)(2,1)S(1)}, bf16[4,64,320]{2,1,0:T(8,128)(2,1)}, u32[]{:S(2)}) copy-start(bf16[4,64,320]{2,1,0:T(8,128)(2,1)} %refs_0_.3) | copy-start | bytes 491524
  9.0 4.6 %collective-permute-start.2 = (bf16[32,320]{1,0:T(8,128)(2,1)S(1)}, bf16[32,320]{1,0:T(8,128)(2,1)S(1)}, u32[]{:S(2)}, u32[]{:S(2)}) collective-permute-start(bf16[32,320]{1,0:T(8,128)(2,1)S(1)} %get-tuple-element.29), channel_id=1, source_target_pairs={{0,1},{1,0},{2,3},{3,2},{4,5},{5,4},{6,7},{7,6},{8,9},{9,8},{10,11... | collective-permute-start | bytes 61448 | tf_op jit(solution)/shard_map/ppermute | solution.py:617
  9.1 4.6 %collective-permute-start.3 = (bf16[32,320]{1,0:T(8,128)(2,1)S(1)}, bf16[32,320]{1,0:T(8,128)(2,1)S(1)}, u32[]{:S(2)}, u32[]{:S(2)}) collective-permute-start(bf16[32,320]{1,0:T(8,128)(2,1)S(1)} %get-tuple-element.30), channel_id=1, source_target_pairs={{1,2},{3,4},{5,6},{7,8},{9,10},{11,12},{13,14},{2,1},{4,3},{6,5},{... | collective-permute-start | bytes 61448 | tf_op jit(solution)/shard_map/ppermute | solution.py:636
  10.2 5.2 %collective-permute-start.1 = (bf16[4,64,320]{2,1,0:T(8,128)(2,1)S(1)}, bf16[4,64,320]{2,1,0:T(8,128)(2,1)S(1)}, u32[]{:S(2)}, u32[]{:S(2)}) collective-permute-start(bf16[4,64,320]{2,1,0:T(8,128)(2,1)S(1)} %shard_map.76.refs_0_), channel_id=1, source_target_pairs={{0,1},{1,0},{2,3},{3,2},{4,5},{5,4},{6,7},{7,6},{8,9},{9,8},{10,11... | collective-permute-start | bytes 491528 | tf_op jit(solution)/shard_map/ppermute | solution.py:617
  13.6 1.7 %copy-start.2 = (bf16[4,64,320]{2,1,0:T(8,128)(2,1)S(1)}, bf16[4,64,320]{2,1,0:T(8,128)(2,1)}, u32[]{:S(2)}) copy-start(bf16[4,64,320]{2,1,0:T(8,128)(2,1)} %refs_1_.5) | copy-start | bytes 491524
  13.6 1.7 %copy-start.5 = (bf16[4,64,320]{2,1,0:T(8,128)(2,1)S(1)}, bf16[4,64,320]{2,1,0:T(8,128)(2,1)}, u32[]{:S(2)}) copy-start(bf16[4,64,320]{2,1,0:T(8,128)(2,1)} %refs_0_.3) | copy-start | bytes 491524
  13.8 6.2 %collective-permute-start.4 = (bf16[6,80,128]{2,1,0:T(8,128)(2,1)S(1)}, bf16[6,80,128]{2,1,0:T(8,128)(2,1)S(1)}, u32[]{:S(2)}, u32[]{:S(2)}) collective-permute-start(bf16[6,80,128]{2,1,0:T(8,128)(2,1)S(1)} %shard_map.79), channel_id=1, source_target_pairs={{0,16},{16,0},{1,17},{17,1},{2,18},{18,2},{3,19},{19,3},{4,20},{20... | collective-permute-start | bytes 368648 | tf_op jit(solution)/shard_map/ppermute | solution.py:572
  22.0 1.4 %collective-permute-start.5 = (f32[192,128]{1,0:T(8,128)S(1)}, f32[192,128]{1,0:T(8,128)S(1)}, u32[]{:S(2)}, u32[]{:S(2)}) collective-permute-start(f32[192,128]{1,0:T(8,128)S(1)} %get-tuple-element.35), channel_id=1, source_target_pairs={{0,1},{1,0},{2,3},{3,2},{4,5},{5,4},{6,7},{7,6},{8,9},{9,8},{10,11... | collective-permute-start | bytes 294920 | tf_op jit(solution)/shard_map/ppermute | solution.py:617
  23.4 6.6 %collective-permute-start.8 = (bf16[192,128]{1,0:T(8,128)(2,1)S(1)}, bf16[192,128]{1,0:T(8,128)(2,1)S(1)}, u32[]{:S(2)}, u32[]{:S(2)}) collective-permute-start(bf16[192,128]{1,0:T(8,128)(2,1)S(1)} %shard_map.81.refs_0_.refs_1_), channel_id=1, source_target_pairs={{0,18},{1,19},{2,16},{3,17},{4,22},{5,23},{6,20},{7,21},{8,26},{9,... | collective-permute-start | bytes 147464 | tf_op jit(solution)/shard_map/ppermute | solution.py:617
  26.2 4.1 %collective-permute-start.7 = (bf16[192,128]{1,0:T(8,128)(2,1)S(1)}, bf16[192,128]{1,0:T(8,128)(2,1)S(1)}, u32[]{:S(2)}, u32[]{:S(2)}) collective-permute-start(bf16[192,128]{1,0:T(8,128)(2,1)S(1)} %shard_map.81.refs_0_.refs_1_), channel_id=1, source_target_pairs={{0,16},{1,17},{2,18},{3,19},{4,20},{5,21},{6,22},{7,23},{8,24},{9,... | collective-permute-start | bytes 147464 | tf_op jit(solution)/shard_map/ppermute | solution.py:617
  26.7 4.1 %collective-permute-start.6 = (bf16[192,128]{1,0:T(8,128)(2,1)S(1)}, bf16[192,128]{1,0:T(8,128)(2,1)S(1)}, u32[]{:S(2)}, u32[]{:S(2)}) collective-permute-start(bf16[192,128]{1,0:T(8,128)(2,1)S(1)} %shard_map.81.refs_0_.refs_1_), channel_id=1, source_target_pairs={{0,2},{1,3},{2,0},{3,1},{4,6},{5,7},{6,4},{7,5},{8,10},{9,11},{10,... | collective-permute-start | bytes 147464 | tf_op jit(solution)/shard_map/ppermute | solution.py:617
  29.9 6.9 %collective-permute-start.9 = (bf16[4,64,320]{2,1,0:T(8,128)(2,1)S(1)}, bf16[4,64,320]{2,1,0:T(8,128)(2,1)S(1)}, u32[]{:S(2)}, u32[]{:S(2)}) collective-permute-start(bf16[4,64,320]{2,1,0:T(8,128)(2,1)S(1)} %get-tuple-element.40), channel_id=1, source_target_pairs={{0,1},{1,0},{2,3},{3,2},{4,5},{5,4},{6,7},{7,6},{8,9},{9,8},{10,11... | collective-permute-start | bytes 491528 | tf_op jit(solution)/shard_map/ppermute | solution.py:617
  30.9 10.0 %collective-permute-start.13 = (bf16[960,128]{1,0:T(8,128)(2,1)S(1)}, bf16[960,128]{1,0:T(8,128)(2,1)S(1)}, u32[]{:S(2)}, u32[]{:S(2)}) collective-permute-start(bf16[960,128]{1,0:T(8,128)(2,1)S(1)} %shard_map.84.refs_0_), channel_id=1, source_target_pairs={{0,16},{16,0},{1,17},{17,1},{2,18},{18,2},{3,19},{19,3},{4,20},{20... | collective-permute-start | bytes 737288 | tf_op jit(solution)/shard_map/ppermute | solution.py:572
  32.4 7.7 %collective-permute-start.12 = (bf16[192,128]{1,0:T(8,128)(2,1)S(1)}, bf16[192,128]{1,0:T(8,128)(2,1)S(1)}, u32[]{:S(2)}, u32[]{:S(2)}) collective-permute-start(bf16[192,128]{1,0:T(8,128)(2,1)S(1)} %shard_map.83.refs_0_.refs_1_), channel_id=1, source_target_pairs={{0,12},{1,13},{2,14},{3,15},{4,8},{5,9},{6,10},{7,11},{8,4},{9,5},... | collective-permute-start | bytes 147464 | tf_op jit(solution)/shard_map/ppermute | solution.py:617
  35.7 5.0 %collective-permute-start.11 = (bf16[192,128]{1,0:T(8,128)(2,1)S(1)}, bf16[192,128]{1,0:T(8,128)(2,1)S(1)}, u32[]{:S(2)}, u32[]{:S(2)}) collective-permute-start(bf16[192,128]{1,0:T(8,128)(2,1)S(1)} %shard_map.83.refs_0_.refs_1_), channel_id=1, source_target_pairs={{0,8},{1,9},{2,10},{3,11},{4,12},{5,13},{6,14},{7,15},{8,0},{9,1},... | collective-permute-start | bytes 147464 | tf_op jit(solution)/shard_map/ppermute | solution.py:617
  35.7 5.0 %collective-permute-start.10 = (bf16[192,128]{1,0:T(8,128)(2,1)S(1)}, bf16[192,128]{1,0:T(8,128)(2,1)S(1)}, u32[]{:S(2)}, u32[]{:S(2)}) collective-permute-start(bf16[192,128]{1,0:T(8,128)(2,1)S(1)} %shard_map.83.refs_0_.refs_1_), channel_id=1, source_target_pairs={{0,4},{1,5},{2,6},{3,7},{4,0},{5,1},{6,2},{7,3},{8,12},{9,13},{10,... | collective-permute-start | bytes 147464 | tf_op jit(solution)/shard_map/ppermute | solution.py:617
  36.9 7.9 %collective-permute-start.15 = (bf16[4,64,320]{2,1,0:T(8,128)(2,1)S(1)}, bf16[4,64,320]{2,1,0:T(8,128)(2,1)S(1)}, u32[]{:S(2)}, u32[]{:S(2)}) collective-permute-start(bf16[4,64,320]{2,1,0:T(8,128)(2,1)S(1)} %shard_map.85.refs_0_), channel_id=1, source_target_pairs={{2,0},{3,1},{4,2},{5,3},{6,4},{7,5},{8,6},{9,7},{10,8},{11,9},{12,... | collective-permute-start | bytes 491528 | tf_op jit(solution)/shard_map/ppermute | solution.py:561
  40.7 4.0 %collective-permute-start.14 = (f32[192,128]{1,0:T(8,128)S(1)}, f32[192,128]{1,0:T(8,128)S(1)}, u32[]{:S(2)}, u32[]{:S(2)}) collective-permute-start(f32[192,128]{1,0:T(8,128)S(1)} %shard_map.87.refs_0_.refs_1_), channel_id=1, source_target_pairs={{0,1},{1,0},{2,3},{3,2},{4,5},{5,4},{6,7},{7,6},{8,9},{9,8},{10,11... | collective-permute-start | bytes 294920 | tf_op jit(solution)/shard_map/ppermute | solution.py:617
